TPU v7x, 512 devices: a whole 4x8x8 slice. The times are simulated.
512 devices in a mesh: gx: 32 (over x, y), gy: 16 (over z, core).
Axes of the slice: x: 4, y: 8, z: 8, core: 2. Of those that a mesh axis runs over, the one named last changes fastest.
Arguments:
- intensity: float32 [4, 4096, 2048], P(None, 'gx', 'gy'), may hold values from -6 to 6
- reach_along_x: float32 [4, 2048], P(None, 'gy'), may hold values from 8 to 16384
- reach_along_y: float32 [4, 4096], P(None, 'gx'), may hold values from 8 to 8192
Outputs:
- smoothed: float32 [4, 4096, 2048], P(None, 'gx', 'gy')
All inputs are finite; a program needn't handle non-finite values.
Results may differ from a plain program's by a relative error of at most 0.00011.
Values sent between devices are 32-bit elements; how exact they have to be, the bound alone decides.
No kernel may reach another device: no remote copies, remote signals or barrier semaphores. Data moves between devices by JAX's collectives and lax.ppermute only.
A program may use at most 128 MiB of HBM per device.

v0:
```python
import jax
import jax.numpy as jnp
from jax import lax
from jax.sharding import PartitionSpec as P

edge_slope = 3.0


def entering(value, axis, combine, identity, reverse):
    size, here = (lax.axis_size(axis), lax.axis_index(axis))
    everything = jax.tree.map(lambda part: lax.all_gather(part, axis), value)
    start = jax.tree.map(
        lambda part, zero: jnp.broadcast_to(jnp.asarray(zero, part.dtype), part.shape),
        value,
        identity,
    )

    def turn(k, before):
        at = size - 1 - k if reverse else k
        reached = at > here if reverse else at < here
        new = combine(before, jax.tree.map(lambda part: part[at], everything))
        return jax.tree.map(lambda a, b: jnp.where(reached, a, b), new, before)

    return lax.fori_loop(0, size, turn, start)


def extended(value, sides, width):
    for axis, dim in sides:
        size, length = (lax.axis_size(axis), value.shape[dim])
        up = [(i, (i + 1) % size) for i in range(size - 1)]
        down = [(j, i) for i, j in up]
        last = lax.slice_in_dim(value, length - width, length, axis=dim)
        first = lax.slice_in_dim(value, 0, width, axis=dim)
        before = lax.ppermute(last, axis, up)
        after = lax.ppermute(first, axis, down)
        value = jnp.concatenate([before, value, after], axis=dim)
    return value


def decay_map(gradient, reach):
    return jnp.exp(-(1.0 + edge_slope * jnp.abs(gradient)) / reach)


def pole_list(decay):
    poles = [decay]
    for level in range(3):
        poles.append(poles[-1] * poles[-1])
    return poles


def combine(earlier, later):
    return (later[0] * earlier[0], later[0] * earlier[1] + later[1])


def local_pass(values, pole, reverse):

    def advance(carried, inputs):
        source, weight = inputs
        output = weight * carried[0] + (1.0 - weight) * source
        product = weight * carried[1]
        return ((output, product), (output, product))

    zeroes = jnp.zeros(values.shape[1:], jnp.float32)
    unity_ones = jnp.ones(values.shape[1:], jnp.float32)
    _, (outputs, products) = lax.scan(
        advance, (zeroes, unity_ones), (values, pole), reverse=reverse
    )
    edge_index = 0 if reverse else values.shape[0] - 1
    block = (products[edge_index], outputs[edge_index])
    neutral = (unity_ones, zeroes)
    return (outputs, products, block, neutral)


def cascade_x(values, decay):
    poles = pole_list(decay)
    for pole in poles:
        outputs, products, block, neutral = local_pass(values, pole, False)
        incoming = entering(block, "gx", combine, neutral, False)
        values = outputs + products * incoming[1][None]
    for pole in poles:
        outputs, products, block, neutral = local_pass(values, pole, True)
        incoming = entering(block, "gx", combine, neutral, True)
        values = outputs + products * incoming[1][None]
    return values


def cascade_y(values, decay):
    poles = pole_list(decay)
    for pole in poles:
        outputs, products, block, neutral = local_pass(values, pole, False)
        incoming = entering(block, "gy", combine, neutral, False)
        values = outputs + products * incoming[1][None]
    for pole in poles:
        outputs, products, block, neutral = local_pass(values, pole, True)
        incoming = entering(block, "gy", combine, neutral, True)
        values = outputs + products * incoming[1][None]
    return values


def per_device(intensity, reach_along_x, reach_along_y):
    padded = extended(intensity, (("gx", 1), ("gy", 2)), 1)
    gradient_x = 0.5 * (padded[:, 2:, 1:-1] - padded[:, :-2, 1:-1])
    gradient_y = 0.5 * (padded[:, 1:-1, 2:] - padded[:, 1:-1, :-2])
    decay_x = decay_map(gradient_x, reach_along_x[:, None, :])
    decay_y = decay_map(gradient_y, reach_along_y[:, :, None])
    lines_x = jnp.transpose(intensity, (1, 0, 2))
    decay_lines = jnp.transpose(decay_x, (1, 0, 2))
    across_x = cascade_x(lines_x, decay_lines)
    lines_y = jnp.transpose(across_x, (2, 1, 0))
    decay_lines_y = jnp.transpose(decay_y, (2, 0, 1))
    across_y = cascade_y(lines_y, decay_lines_y)
    return jnp.transpose(across_y, (1, 2, 0))


def solution(mesh):
    return jax.shard_map(
        per_device,
        mesh=mesh,
        in_specs=(P(None, "gx", "gy"), P(None, "gy"), P(None, "gx")),
        out_specs=P(None, "gx", "gy"),
        check_vma=False,
    )
```

profile of v0, /device:TPU:1, one launch (start us, length us, event | category | flops | bytes accessed | tf_op | source)
XLA Modules:
  0.0 1131.5 jit_solution(13160827199159296085)
XLA Ops:
  18.3 39.4 %all_gather.96 = f32[32,4,128]{2,1,0:T(4,128)S(1)} all-gather(f32[1,4,128]{2,1,0:T(4,128)S(1)} %slice.132), channel_id=1, replica_groups=mesh['gx'=32,'gy'=16] {'gx'}, dimensions={0}, use_global_device_ids=true | all-gather | bytes 67584 | tf_op jit(solution)/shard_map/all_gather | solution.py:11
  57.7 35.9 %all_gather.97 = f32[32,4,128]{2,1,0:T(4,128)S(1)} all-gather(f32[1,4,128]{2,1,0:T(4,128)S(1)} %slice.133), channel_id=1, replica_groups=mesh['gx'=32,'gy'=16] {'gx'}, dimensions={0}, use_global_device_ids=true | all-gather | bytes 67584 | tf_op jit(solution)/shard_map/all_gather | solution.py:11
  100.3 34.0 %all_gather.98 = f32[32,4,128]{2,1,0:T(4,128)S(1)} all-gather(f32[1,4,128]{2,1,0:T(4,128)S(1)} %slice.134), channel_id=1, replica_groups=mesh['gx'=32,'gy'=16] {'gx'}, dimensions={0}, use_global_device_ids=true | all-gather | bytes 67584 | tf_op jit(solution)/shard_map/all_gather | solution.py:11
  134.3 35.6 %all_gather.99 = f32[32,4,128]{2,1,0:T(4,128)S(1)} all-gather(f32[1,4,128]{2,1,0:T(4,128)S(1)} %slice.135), channel_id=1, replica_groups=mesh['gx'=32,'gy'=16] {'gx'}, dimensions={0}, use_global_device_ids=true | all-gather | bytes 67584 | tf_op jit(solution)/shard_map/all_gather | solution.py:11
  176.6 34.3 %all_gather.100 = f32[32,4,128]{2,1,0:T(4,128)S(1)} all-gather(f32[1,4,128]{2,1,0:T(4,128)S(1)} %slice.136), channel_id=1, replica_groups=mesh['gx'=32,'gy'=16] {'gx'}, dimensions={0}, use_global_device_ids=true | all-gather | bytes 67584 | tf_op jit(solution)/shard_map/all_gather | solution.py:11
  210.9 35.6 %all_gather.101 = f32[32,4,128]{2,1,0:T(4,128)S(1)} all-gather(f32[1,4,128]{2,1,0:T(4,128)S(1)} %slice.137), channel_id=1, replica_groups=mesh['gx'=32,'gy'=16] {'gx'}, dimensions={0}, use_global_device_ids=true | all-gather | bytes 67584 | tf_op jit(solution)/shard_map/all_gather | solution.py:11
  253.2 34.3 %all_gather.102 = f32[32,4,128]{2,1,0:T(4,128)S(1)} all-gather(f32[1,4,128]{2,1,0:T(4,128)S(1)} %slice.138), channel_id=1, replica_groups=mesh['gx'=32,'gy'=16] {'gx'}, dimensions={0}, use_global_device_ids=true | all-gather | bytes 67584 | tf_op jit(solution)/shard_map/all_gather | solution.py:11
  287.5 35.3 %all_gather.103 = f32[32,4,128]{2,1,0:T(4,128)S(1)} all-gather(f32[1,4,128]{2,1,0:T(4,128)S(1)} %slice.139), channel_id=1, replica_groups=mesh['gx'=32,'gy'=16] {'gx'}, dimensions={0}, use_global_device_ids=true | all-gather | bytes 67584 | tf_op jit(solution)/shard_map/all_gather | solution.py:11
  329.1 34.4 %all_gather.104 = f32[32,4,128]{2,1,0:T(4,128)S(1)} all-gather(f32[1,4,128]{2,1,0:T(4,128)S(1)} %slice.140), channel_id=1, replica_groups=mesh['gx'=32,'gy'=16] {'gx'}, dimensions={0}, use_global_device_ids=true | all-gather | bytes 67584 | tf_op jit(solution)/shard_map/all_gather | solution.py:11
  363.6 35.0 %all_gather.105 = f32[32,4,128]{2,1,0:T(4,128)S(1)} all-gather(f32[1,4,128]{2,1,0:T(4,128)S(1)} %slice.141), channel_id=1, replica_groups=mesh['gx'=32,'gy'=16] {'gx'}, dimensions={0}, use_global_device_ids=true | all-gather | bytes 67584 | tf_op jit(solution)/shard_map/all_gather | solution.py:11
  405.1 34.7 %all_gather.106 = f32[32,4,128]{2,1,0:T(4,128)S(1)} all-gather(f32[1,4,128]{2,1,0:T(4,128)S(1)} %slice.142), channel_id=1, replica_groups=mesh['gx'=32,'gy'=16] {'gx'}, dimensions={0}, use_global_device_ids=true | all-gather | bytes 67584 | tf_op jit(solution)/shard_map/all_gather | solution.py:11
  439.8 35.0 %all_gather.107 = f32[32,4,128]{2,1,0:T(4,128)S(1)} all-gather(f32[1,4,128]{2,1,0:T(4,128)S(1)} %slice.143), channel_id=1, replica_groups=mesh['gx'=32,'gy'=16] {'gx'}, dimensions={0}, use_global_device_ids=true | all-gather | bytes 67584 | tf_op jit(solution)/shard_map/all_gather | solution.py:11
  481.3 34.5 %all_gather.108 = f32[32,4,128]{2,1,0:T(4,128)S(1)} all-gather(f32[1,4,128]{2,1,0:T(4,128)S(1)} %slice.144), channel_id=1, replica_groups=mesh['gx'=32,'gy'=16] {'gx'}, dimensions={0}, use_global_device_ids=true | all-gather | bytes 67584 | tf_op jit(solution)/shard_map/all_gather | solution.py:11
  515.9 34.8 %all_gather.109 = f32[32,4,128]{2,1,0:T(4,128)S(1)} all-gather(f32[1,4,128]{2,1,0:T(4,128)S(1)} %slice.145), channel_id=1, replica_groups=mesh['gx'=32,'gy'=16] {'gx'}, dimensions={0}, use_global_device_ids=true | all-gather | bytes 67584 | tf_op jit(solution)/shard_map/all_gather | solution.py:11
  557.2 35.2 %all_gather.110 = f32[32,4,128]{2,1,0:T(4,128)S(1)} all-gather(f32[1,4,128]{2,1,0:T(4,128)S(1)} %slice.146), channel_id=1, replica_groups=mesh['gx'=32,'gy'=16] {'gx'}, dimensions={0}, use_global_device_ids=true | all-gather | bytes 67584 | tf_op jit(solution)/shard_map/all_gather | solution.py:11
  592.5 34.5 %all_gather.111 = f32[32,4,128]{2,1,0:T(4,128)S(1)} all-gather(f32[1,4,128]{2,1,0:T(4,128)S(1)} %slice.147), channel_id=1, replica_groups=mesh['gx'=32,'gy'=16] {'gx'}, dimensions={0}, use_global_device_ids=true | all-gather | bytes 67584 | tf_op jit(solution)/shard_map/all_gather | solution.py:11
  628.5 199.7 %collective-permute-start.2 = (f32[4,130,1]{1,0,2:T(4,128)S(1)}, f32[4,130,1]{1,0,2:T(4,128)S(1)}, u32[]{:S(2)}, u32[]{:S(2)}) collective-permute-start(f32[4,130,1]{1,0,2:T(4,128)S(1)} %get-tuple-element.4632), channel_id=1, source_target_pairs={{1,0},{2,1},{3,2},{4,3},{5,4},{6,5},{7,6},{8,7},{9,8},{10,9},{11,1... | collective-permute-start | bytes 6248 | tf_op jit(solution)/shard_map/ppermute | solution.py:35
  838.4 23.4 %all_gather.112 = f32[16,4,128]{2,1,0:T(4,128)S(1)} all-gather(f32[1,4,128]{2,1,0:T(4,128)S(1)} %slice.148), channel_id=1, replica_groups=mesh['gx'=32,'gy'=16] {'gy'}, dimensions={0}, use_global_device_ids=true | all-gather | bytes 34816 | tf_op jit(solution)/shard_map/all_gather | solution.py:11
  861.8 14.5 %all_gather.113 = f32[16,4,128]{2,1,0:T(4,128)S(1)} all-gather(f32[1,4,128]{2,1,0:T(4,128)S(1)} %slice.149), channel_id=1, replica_groups=mesh['gx'=32,'gy'=16] {'gy'}, dimensions={0}, use_global_device_ids=true | all-gather | bytes 34816 | tf_op jit(solution)/shard_map/all_gather | solution.py:11
  882.2 15.9 %all_gather.114 = f32[16,4,128]{2,1,0:T(4,128)S(1)} all-gather(f32[1,4,128]{2,1,0:T(4,128)S(1)} %slice.150), channel_id=1, replica_groups=mesh['gx'=32,'gy'=16] {'gy'}, dimensions={0}, use_global_device_ids=true | all-gather | bytes 34816 | tf_op jit(solution)/shard_map/all_gather | solution.py:11
  898.1 14.5 %all_gather.115 = f32[16,4,128]{2,1,0:T(4,128)S(1)} all-gather(f32[1,4,128]{2,1,0:T(4,128)S(1)} %slice.151), channel_id=1, replica_groups=mesh['gx'=32,'gy'=16] {'gy'}, dimensions={0}, use_global_device_ids=true | all-gather | bytes 34816 | tf_op jit(solution)/shard_map/all_gather | solution.py:11
  918.5 15.9 %all_gather.116 = f32[16,4,128]{2,1,0:T(4,128)S(1)} all-gather(f32[1,4,128]{2,1,0:T(4,128)S(1)} %slice.152), channel_id=1, replica_groups=mesh['gx'=32,'gy'=16] {'gy'}, dimensions={0}, use_global_device_ids=true | all-gather | bytes 34816 | tf_op jit(solution)/shard_map/all_gather | solution.py:11
  934.4 14.5 %all_gather.117 = f32[16,4,128]{2,1,0:T(4,128)S(1)} all-gather(f32[1,4,128]{2,1,0:T(4,128)S(1)} %slice.153), channel_id=1, replica_groups=mesh['gx'=32,'gy'=16] {'gy'}, dimensions={0}, use_global_device_ids=true | all-gather | bytes 34816 | tf_op jit(solution)/shard_map/all_gather | solution.py:11
  954.7 15.9 %all_gather.118 = f32[16,4,128]{2,1,0:T(4,128)S(1)} all-gather(f32[1,4,128]{2,1,0:T(4,128)S(1)} %slice.154), channel_id=1, replica_groups=mesh['gx'=32,'gy'=16] {'gy'}, dimensions={0}, use_global_device_ids=true | all-gather | bytes 34816 | tf_op jit(solution)/shard_map/all_gather | solution.py:11
  970.6 14.5 %all_gather.119 = f32[16,4,128]{2,1,0:T(4,128)S(1)} all-gather(f32[1,4,128]{2,1,0:T(4,128)S(1)} %slice.155), channel_id=1, replica_groups=mesh['gx'=32,'gy'=16] {'gy'}, dimensions={0}, use_global_device_ids=true | all-gather | bytes 34816 | tf_op jit(solution)/shard_map/all_gather | solution.py:11
  990.8 15.9 %all_gather.120 = f32[16,4,128]{2,1,0:T(4,128)S(1)} all-gather(f32[1,4,128]{2,1,0:T(4,128)S(1)} %slice.156), channel_id=1, replica_groups=mesh['gx'=32,'gy'=16] {'gy'}, dimensions={0}, use_global_device_ids=true | all-gather | bytes 34816 | tf_op jit(solution)/shard_map/all_gather | solution.py:11
  1006.7 14.5 %all_gather.121 = f32[16,4,128]{2,1,0:T(4,128)S(1)} all-gather(f32[1,4,128]{2,1,0:T(4,128)S(1)} %slice.157), channel_id=1, replica_groups=mesh['gx'=32,'gy'=16] {'gy'}, dimensions={0}, use_global_device_ids=true | all-gather | bytes 34816 | tf_op jit(solution)/shard_map/all_gather | solution.py:11
  1027.0 15.9 %all_gather.122 = f32[16,4,128]{2,1,0:T(4,128)S(1)} all-gather(f32[1,4,128]{2,1,0:T(4,128)S(1)} %slice.158), channel_id=1, replica_groups=mesh['gx'=32,'gy'=16] {'gy'}, dimensions={0}, use_global_device_ids=true | all-gather | bytes 34816 | tf_op jit(solution)/shard_map/all_gather | solution.py:11
  1042.8 14.5 %all_gather.123 = f32[16,4,128]{2,1,0:T(4,128)S(1)} all-gather(f32[1,4,128]{2,1,0:T(4,128)S(1)} %slice.159), channel_id=1, replica_groups=mesh['gx'=32,'gy'=16] {'gy'}, dimensions={0}, use_global_device_ids=true | all-gather | bytes 34816 | tf_op jit(solution)/shard_map/all_gather | solution.py:11
  1063.1 15.9 %all_gather.124 = f32[16,4,128]{2,1,0:T(4,128)S(1)} all-gather(f32[1,4,128]{2,1,0:T(4,128)S(1)} %slice.160), channel_id=1, replica_groups=mesh['gx'=32,'gy'=16] {'gy'}, dimensions={0}, use_global_device_ids=true | all-gather | bytes 34816 | tf_op jit(solution)/shard_map/all_gather | solution.py:11
  1079.0 14.5 %all_gather.125 = f32[16,4,128]{2,1,0:T(4,128)S(1)} all-gather(f32[1,4,128]{2,1,0:T(4,128)S(1)} %slice.161), channel_id=1, replica_groups=mesh['gx'=32,'gy'=16] {'gy'}, dimensions={0}, use_global_device_ids=true | all-gather | bytes 34816 | tf_op jit(solution)/shard_map/all_gather | solution.py:11
  1099.6 15.9 %all_gather.126 = f32[16,4,128]{2,1,0:T(4,128)S(1)} all-gather(f32[1,4,128]{2,1,0:T(4,128)S(1)} %slice.162), channel_id=1, replica_groups=mesh['gx'=32,'gy'=16] {'gy'}, dimensions={0}, use_global_device_ids=true | all-gather | bytes 34816 | tf_op jit(solution)/shard_map/all_gather | solution.py:11
  (2637 shorter events, 178.7 us)
Async XLA Ops:
  0.7 5.7 copy-start
  0.9 7.5 collective-permute-start
  5.1 7.1 collective-permute-start.1
  7.2 0.7 copy-start.2
  628.5 203.8 %collective-permute-start.2 = (f32[4,130,1]{1,0,2:T(4,128)S(1)}, f32[4,130,1]{1,0,2:T(4,128)S(1)}, u32[]{:S(2)}, u32[]{:S(2)}) collective-permute-start(f32[4,130,1]{1,0,2:T(4,128)S(1)} %get-tuple-element.4632), channel_id=1, source_target_pairs={{1,0},{2,1},{3,2},{4,3},{5,4},{6,5},{7,6},{8,7},{9,8},{10,9},{11,1... | collective-permute-start | bytes 6248 | tf_op jit(solution)/shard_map/ppermute | solution.py:35
  828.2 4.6 collective-permute-start.3
  832.2 0.7 copy-start.1
where the time goes:
time: 1130 us
  blocking collectives  813 us (72%)
  starting transfers between devices  209 us (18%)
  other arithmetic  49.7 us (4%)
  loops' own time  48.8 us (4%)
    all_gather x32, blocking collectives, entering(): everything = jax.tree.map(lambda part: lax.all_gather(part, axis), value)  813 us
    ppermute x2, starting transfers between devices, extended(): after = lax.ppermute(first, axis, down)  201 us
    dynamic_update_slice x2048, other arithmetic, local_pass(): lax.scan(advance, (zeroes, unity_ones), (values, pole), reverse=reverse)  41 us
    another operation x16, loops' own time, local_pass(): lax.scan(advance, (zeroes, unity_ones), (values, pole), reverse=reverse)  39.3 us
  transfers between devices with their start and end apart: 4, of which 3 were waited for; matrix products, arithmetic and copies ran while one was open for 0% of the time, Pallas kernels for 0%

commit v1 on v0

v1 whole, which is shorter than its diff:
```python
import functools

import jax
import jax.numpy as jnp
from jax import lax
from jax.experimental import pallas as pl
from jax.experimental.pallas import tpu as pltpu
from jax.sharding import PartitionSpec as P

edge_slope = 3.0

LOWER = [(k, j) for k in range(4) for j in range(k + 1)]
BELOW = [(k, j) for k in range(4) for j in range(k)]
FULL = [(k, j) for k in range(4) for j in range(4)]
VALUES = 37

params = pltpu.CompilerParams(vmem_limit_bytes=48 * 1024 * 1024)
MATRICES = 29
SLOTS = 48
APART = 9


def unpack_matrices(get):
    A, B = {}, {}
    for n, kj in enumerate(BELOW):
        A[kj], B[kj] = get(1 + n), get(7 + n)
    power = get(0)
    for k in range(4):
        A[k, k] = B[k, k] = power
        power = power * power
    return A, B, {kj: get(13 + n) for n, kj in enumerate(FULL)}


def pack_matrices(matrices):
    A, B, C = matrices
    return [A[0, 0]] + [A[kj] for kj in BELOW] + [B[kj] for kj in BELOW] + [C[kj] for kj in FULL]


def unpack(get):
    A, B, C = unpack_matrices(get)
    vectors = [get(MATRICES + n) for n in range(8)]
    return A, vectors[:4], B, C, vectors[4:]


def pack(block):
    A, u, B, C, w = block
    return pack_matrices((A, B, C)) + list(u) + list(w)


def total(terms):
    terms = list(terms)
    while len(terms) > 1:
        terms = [a + b for a, b in zip(terms[::2], terms[1::2])] + terms[len(terms) - len(terms) % 2 :]
    return terms[0]


def lower_times(M, x):
    return [total([M[k, j] * x[j] for j in range(k + 1)]) for k in range(4)]


def full_times(M, x):
    return [total([M[k, j] * x[j] for j in range(4)]) for k in range(4)]


def plus(x, y):
    return [a + b for a, b in zip(x, y)]


def lower_product(M, N):
    return {(k, j): total([M[k, i] * N[i, j] for i in range(j, k + 1)]) for k, j in LOWER}


def compose_matrices(left, right):
    A1, B1, C1 = left
    A2, B2, C2 = right
    A = lower_product(A2, A1)
    B = lower_product(B1, B2)
    CA = {(k, j): total([C2[k, i] * A1[i, j] for i in range(j, 4)]) for k, j in FULL}
    C = {(k, j): total([B1[k, i] * CA[i, j] for i in range(k + 1)]) + C1[k, j] for k, j in FULL}
    return A, B, C


def compose_vectors(B1, A2, C2, left, right):
    u1, w1 = left
    u2, w2 = right
    u = plus(lower_times(A2, u1), u2)
    w = plus(lower_times(B1, plus(full_times(C2, u1), w2)), w1)
    return u, w


def compose(left, right):
    A1, u1, B1, C1, w1 = left
    A2, u2, B2, C2, w2 = right
    A, B, C = compose_matrices((A1, B1, C1), (A2, B2, C2))
    u, w = compose_vectors(B1, A2, C2, (u1, w1), (u2, w2))
    return A, u, B, C, w


def forward_out(block, f):
    A, u = block[:2]
    return [total([A[k, j] * f[j] for j in range(k + 1)] + [u[k]]) for k in range(4)]


def backward_out(block, f, b):
    B, C, w = block[2:]
    return [total([B[k, j] * b[j] for j in range(k + 1)] + [C[k, j] * f[j] for j in range(4)] + [w[k]]) for k in range(4)]


def poles_of(d):
    p = [d]
    for _ in range(3):
        p.append(p[-1] * p[-1])
    return p, [1.0 - x for x in p]


STEPS, UNROLL = 64, 8
PITCH = 65
padded = (8 * PITCH, 128)


def loop(body, carry, reverse=False):
    def some(n, carry):
        for k in range(UNROLL):
            at = n * UNROLL + k
            carry = body(STEPS - 1 - at if reverse else at, carry)
        return carry

    return lax.fori_loop(0, STEPS // UNROLL, some, carry)


def rows(s):
    return pl.ds(s, 8, stride=PITCH)


def decay_block(v, inverse):
    at = lax.broadcasted_iota(jnp.int32, v.shape, 0)
    n = v.shape[0]
    gradient = 0.5 * (pltpu.roll(v, n - 1, 0) - pltpu.roll(v, 1, 0))
    d = jnp.exp((1.0 + edge_slope * jnp.abs(gradient)) * inverse)
    return jnp.where((at == 0) | (at == n - 1), 1.0, d)


def cascade_lower(p, q, M):
    M = dict(M)
    for j in range(4):
        M[j, j] = p[j] * M[j, j]
        for k in range(j + 1, 4):
            M[k, j] = p[k] * M[k, j] + q[k] * M[k - 1, j]
    return M


def cascade_source(p, q, x, source):
    x = list(x)
    for k in range(4):
        x[k] = p[k] * x[k] + q[k] * (source if k == 0 else x[k - 1])
    return x


def before_step(p, q, B):
    new, inner = {}, []
    for k in range(4):
        carried = B[k, k]
        new[k, k] = p[k] * carried
        for j in reversed(range(k)):
            carried = B[k, j] + q[j + 1] * carried
            new[k, j] = p[j] * carried
        inner.append(q[0] * carried)
    return new, inner


def half_maps(v_ref, d_ref):
    one, zero = jnp.ones((8, 128), jnp.float32), jnp.zeros((8, 128), jnp.float32)

    def step(s, carry):
        A, u, B, C, w = carry
        A, B = dict(zip(LOWER, A)), dict(zip(LOWER, B))
        p, q = poles_of(d_ref[rows(s), :])
        u = cascade_source(p, q, u, v_ref[rows(s), :])
        A = cascade_lower(p, q, A)
        B, inner = before_step(p, q, B)
        C = [c + inner[k] * A[3, j] for c, (k, j) in zip(C, FULL)]
        w = [x + y * u[3] for x, y in zip(w, inner)]
        return [A[kj] for kj in LOWER], u, [B[kj] for kj in LOWER], C, w

    start = [one if k == j else zero for k, j in LOWER]
    A, u, B, C, w = loop(step, (start, [zero] * 4, start, [zero] * 16, [zero] * 4))
    return dict(zip(LOWER, A)), u, dict(zip(LOWER, B)), dict(zip(FULL, C)), w


def after(part):
    if isinstance(part, dict):
        return {key: pltpu.roll(x, 7, 0) for key, x in part.items()}
    return [pltpu.roll(x, 7, 0) for x in part]


def planes():
    return [slice(z * 128, (z + 1) * 128) for z in range(4)]


def place(i):
    return pl.ds(i // STEPS * PITCH + i % STEPS, 4, stride=2 * PITCH)


def spread(ref, z, block):
    for h in range(2):
        at = (2 * z + h) * PITCH
        ref[at : at + STEPS, :] = block[h * STEPS : (h + 1) * STEPS]


def gather(ref, z):
    at = 2 * z * PITCH
    return jnp.concatenate([ref[at : at + STEPS, :], ref[at + PITCH : at + PITCH + STEPS, :]], axis=0)


def swap(x, groups):
    row, lane = (lax.broadcasted_iota(jnp.int32, x.shape, axis) for axis in range(2))
    width = 128 // groups
    t = 1
    while t < groups:
        lower, right = (row // t) % 2 == 1, (lane // (width * t)) % 2 == 1
        up = pltpu.roll(pltpu.roll(x, 8 - t, 0), width * t, 1)
        down = pltpu.roll(pltpu.roll(x, t, 0), 128 - width * t, 1)
        x = jnp.where(lower == right, x, jnp.where(lower, down, up))
        t *= 2
    return x


def summarise(v_ref, source_ref, reach_ref, d_ref, half_ref, chunks_ref, pair_ref):
    for z, here in enumerate(planes()):
        spread(d_ref, z, decay_block(v_ref[here, :], -1.0 / reach_ref[z : z + 1, :]))
    block = half_maps(source_ref, d_ref)
    for n, value in enumerate(pack(block)):
        half_ref[n] = value
    for n, value in enumerate(pack(compose(block, tuple(after(part) for part in block)))):
        pair_ref[n * APART : n * APART + 8, :] = value
    ends = [v_ref[pl.ds(i, 4, stride=128), :] for i in (0, 1, 126, 127)] + [source_ref[place(0), :], source_ref[place(127), :], reach_ref[...]]
    for n, value in enumerate(ends):
        pair_ref[pl.ds((37 + n) * APART, 4, stride=2), :] = value
    for n in range(44, SLOTS):
        pair_ref[n * APART : n * APART + 8, :] = jnp.zeros((8, 128), jnp.float32)
    per_plane = chunks_ref.shape[0] // 4
    groups = per_plane
    for z in range(4):
        chunks = slice(z * per_plane, (z + 1) * per_plane)
        for n in range(0, SLOTS, 8):
            x = swap(pair_ref[pl.ds(n * APART + 2 * z, 8, stride=APART), :], groups)
            for a in range(8 // groups):
                chunks_ref[chunks, n // groups + a, :] = x[a * groups : (a + 1) * groups]


def finish(v_ref, half_ref, state_ref, d_ref, c_ref, out_ref, wide_ref):
    groups = state_ref.shape[0] // 4
    count = 8 // groups
    for z in range(4):
        chunks = slice(z * groups, (z + 1) * groups)
        x = swap(jnp.concatenate([state_ref[chunks, a, :] for a in range(count)], axis=0), groups)
        wide_ref[pl.ds(2 * z, 8, stride=APART), :] = x
        wide_ref[pl.ds(2 * z + 1, 8, stride=APART), :] = x
        x = swap(jnp.concatenate([state_ref[chunks, count, :]] * count, axis=0), groups)
        first, last = 2 * z * PITCH, (2 * z + 1) * PITCH + STEPS - 1
        d_ref[first : first + 1, :] = x[0:1]
        d_ref[last : last + 1, :] = x[1:2]
    f = [wide_ref[k * APART : k * APART + 8, :] for k in range(4)]
    b = [wide_ref[k * APART : k * APART + 8, :] for k in range(4, 8)]
    block = unpack(lambda n: half_ref[n])
    second = lax.broadcasted_iota(jnp.int32, (8, 128), 0) % 2 == 1
    p, q = poles_of(d_ref[rows(0), :])
    f_middle = [pltpu.roll(x, 1, 0) for x in forward_out(block, cascade_source(p, q, f, v_ref[rows(0), :]))]
    p, q = poles_of(d_ref[rows(STEPS - 1), :])
    f_last = cascade_source(p, q, forward_out(block, f_middle), v_ref[rows(STEPS - 1), :])
    b_middle = [pltpu.roll(x, 7, 0) for x in backward_out(block, f_middle, cascade_source(p, q, b, f_last[3]))]
    f = [jnp.where(second, x, y) for x, y in zip(f_middle, f)]
    b = [jnp.where(second, y, x) for x, y in zip(b_middle, b)]

    def forward(s, f):
        p, q = poles_of(d_ref[rows(s), :])
        f = cascade_source(p, q, f, v_ref[rows(s), :])
        c_ref[s] = f[3]
        return f

    loop(forward, f)

    def backward(s, b):
        p, q = poles_of(d_ref[rows(s), :])
        b = cascade_source(p, q, b, c_ref[s])
        out_ref[rows(s), :] = b[3]
        return b

    loop(backward, b, reverse=True)


def x_first(arguments_ref, vt_ref, y_reach_ref, source_ref, d_ref, half_ref, chunks_ref, reach_ref, pair_ref):
    for z, here in enumerate(planes()):
        vt_ref[here, :] = arguments_ref[here, :].T
        spread(source_ref, z, arguments_ref[here, :])
    reach_ref[...] = arguments_ref[512:516, :]
    y_reach_ref[...] = arguments_ref[516:520, :]
    summarise(arguments_ref, source_ref, reach_ref, d_ref, half_ref, chunks_ref, pair_ref)


def x_second_y_first(
    vt_ref, reach_ref, source_ref, dx_ref, xhalf_ref, state_ref,
    t_ref, d_ref, half_ref, chunks_ref,
    ends_ref, c_ref, across_ref, wide_ref, pair_ref,
):
    ends_ref[...] = dx_ref[...]
    finish(source_ref, xhalf_ref, state_ref, ends_ref, c_ref, across_ref, wide_ref)
    for z in range(4):
        spread(t_ref, z, gather(across_ref, z).T)
    summarise(vt_ref, t_ref, reach_ref, d_ref, half_ref, chunks_ref, pair_ref)


def y_second(t_ref, d_ref, half_ref, state_ref, out_ref, ends_ref, c_ref, done_ref, wide_ref):
    ends_ref[...] = d_ref[...]
    finish(t_ref, half_ref, state_ref, ends_ref, c_ref, done_ref, wide_ref)
    for z, here in enumerate(planes()):
        out_ref[here, :] = gather(done_ref, z).T


def with_ends(block, first, last, source_first, source_last):
    A, u, B, C, w = block
    one, zero = jnp.ones_like(first), jnp.zeros_like(first)
    identity = {(k, j): one if k == j else zero for k, j in LOWER}
    p, q = poles_of(last)
    A, u = cascade_lower(p, q, A), cascade_source(p, q, u, source_last)
    inner = lower_times(B, cascade_source(p, q, [zero] * 4, one))
    B = lower_product(B, cascade_lower(p, q, identity))
    C = {(k, j): C[k, j] + inner[k] * A[3, j] for k, j in FULL}
    w = [x + y * u[3] for x, y in zip(w, inner)]
    p, q = poles_of(first)
    T, t = cascade_lower(p, q, identity), cascade_source(p, q, [zero] * 4, source_first)
    w = plus(w, full_times(C, t))
    u = plus(u, lower_times(A, t))
    A = lower_product(A, T)
    C = {(k, j): total([C[k, i] * T[i, j] for i in range(j, 4)]) for k, j in FULL}
    columns = [cascade_source(p, q, [C[k, j] for k in range(4)], T[3, j]) for j in range(4)]
    C = {(k, j): columns[j][k] for k, j in FULL}
    w = cascade_source(p, q, w, t[3])
    B = cascade_lower(p, q, B)
    return A, u, B, C, w


def line_scan(groups, blocks_ref, state_ref, map_ref, f_ref, b_ref):
    count, width = blocks_ref.shape[0], 128 // groups
    eights = count // 8
    row = lax.broadcasted_iota(jnp.int32, (8, 128), 0)
    group = lax.broadcasted_iota(jnp.int32, (8, 128), 1) // width

    def moved(x, by):
        by = by * width % 128
        return pltpu.roll(x, by, 1) if by else x

    def value(n):
        parts = [moved(blocks_ref[8 * g : 8 * g + 8, n // groups, :], g - n % groups) for g in range(eights)]
        x = parts[0]
        for g in range(1, eights):
            x = jnp.where(group == g, parts[g], x)
        return x

    v = [value(37 + n) for n in range(4)]
    below = pltpu.roll(v[3], 1, 0)
    below = jnp.where(row == 0, jnp.where(group == 0, 0.0, moved(below, 1)), below)
    above = pltpu.roll(v[0], 7, 0)
    above = jnp.where(row == 7, jnp.where(group == eights - 1, 0.0, moved(above, -1)), above)
    inverse = -1.0 / value(43)
    first, last = (
        jnp.exp((1.0 + edge_slope * jnp.abs(gradient)) * inverse) for gradient in (0.5 * (v[1] - below), 0.5 * (above - v[2]))
    )
    block = with_ends(unpack(value), first, last, value(41), value(42))
    for n, x in enumerate(pack(block)):
        map_ref[n] = x

    def block_at(m):
        return unpack(lambda n: map_ref[n, m : m + 1, :])

    for reach in (1, 2, 4):
        other = tuple(
            {key: pltpu.roll(x, 8 - reach, 0) for key, x in part.items()} if isinstance(part, dict) else [pltpu.roll(x, 8 - reach, 0) for x in part]
            for part in block
        )
        block = compose(block, other)
    joined = unpack(lambda n, values=pack(block): values[n][0:1])

    here = group[0:1]
    zero = [jnp.zeros((1, 128), jnp.float32)] * 4
    f = zero
    for g in range(1, eights):
        through = [moved(x, 1) for x in forward_out(joined, f)]
        f = [jnp.where(here == g, x, y) for x, y in zip(through, f)]
    b = zero
    for g in reversed(range(eights - 1)):
        through = [moved(x, -1) for x in backward_out(joined, f, b)]
        b = [jnp.where(here == g, x, y) for x, y in zip(through, b)]

    inside = []
    for m in range(8):
        for k in range(4):
            f_ref[k, m : m + 1, :] = f[k]
        inside.append(f)
        f = forward_out(block_at(m), f)
    for m in reversed(range(8)):
        for k in range(4):
            b_ref[k, m : m + 1, :] = b[k]
        b = backward_out(block_at(m), inside[m], b)

    back = [f_ref[k] for k in range(4)] + [b_ref[k] for k in range(4)] + [first, last]
    for g in range(eights):
        some = slice(8 * g, 8 * g + 8)
        for start in range(0, 10, groups):
            x = moved(back[start], -g)
            for n in range(1, min(groups, 10 - start)):
                x = jnp.where(group == n, moved(back[start + n], n - g), x)
            state_ref[some, start // groups, :] = x
    for r in range(-(-10 // groups), state_ref.shape[1]):
        state_ref[:, r, :] = jnp.zeros((count, 128), jnp.float32)


f32 = lambda *shape: jax.ShapeDtypeStruct(shape, jnp.float32)
vmem = lambda *shape: pltpu.VMEM(shape, jnp.float32)
plane = (512, 128)


def call(kernel, out_shape, scratch, *operands):
    return pl.pallas_call(kernel, out_shape=out_shape, scratch_shapes=scratch, compiler_params=params)(*operands)


def states(chunks, axis):
    size = lax.axis_size(axis)
    groups = size // 4
    chunks = lax.all_to_all(chunks, axis, 0, 0, tiled=True)
    scratch = [vmem(37, 8, 128), vmem(4, 8, 128), vmem(4, 8, 128)]
    entering = call(functools.partial(line_scan, groups), f32(size, 16 // groups, 128), scratch, chunks)
    return lax.all_to_all(entering, axis, 0, 0, tiled=True)


def per_device(intensity, reach_along_x, reach_along_y):
    def maps(axis):
        size = lax.axis_size(axis)
        return [f32(*padded), f32(37, 8, 128), f32(size, 256 // size, 128)]

    work = [vmem(SLOTS * APART, 128)]
    ending = [vmem(*padded), vmem(STEPS, 8, 128), vmem(*padded), vmem(8 * APART, 128)]
    vt, y_reach, source, dx, x_half, x_chunks = call(
        x_first, [f32(*plane), f32(4, 128), f32(*padded)] + maps("gx"), [vmem(4, 128)] + work,
        jnp.concatenate([intensity.reshape(plane), reach_along_x, reach_along_y]),
    )
    x_states = states(x_chunks, "gx")
    t, dy, y_half, y_chunks = call(
        x_second_y_first, [f32(*padded)] + maps("gy"), ending + work, vt, y_reach, source, dx, x_half, x_states
    )
    y_states = states(y_chunks, "gy")
    out = call(y_second, f32(*plane), ending, t, dy, y_half, y_states)
    return out.reshape(4, 128, 128)


def solution(mesh):
    return jax.shard_map(
        per_device,
        mesh=mesh,
        in_specs=(P(None, "gx", "gy"), P(None, "gy"), P(None, "gx")),
        out_specs=P(None, "gx", "gy"),
        check_vma=False,
    )
```

time: 1130 us -> 71.9 us (0.06)
  blocking collectives: 813 us -> 64.1 us
  starting transfers between devices: 209 us -> 0 us
  loops' own time: 48.8 us -> 0 us
  other arithmetic: 49.7 us -> 1 us
    all_gather x32 -> x0, blocking collectives: 813 us -> none  [entering(): everything = jax.tree.map(lambda part: lax.all_gather(part, axis), value)]
    ppermute x4 -> x0, starting transfers between devices: 209 us -> none  [the longest x2 201 us: extended(): after = lax.ppermute(first, axis, down)]
    all_to_all x0 -> x4, blocking collectives: none -> 64.1 us  [the longest x2 42 us: states(): chunks = lax.all_to_all(chunks, axis, 0, 0, tiled=True)]
    another operation x32 -> x0, loops' own time: 48.8 us -> none  [the longest x16 39.3 us: local_pass(): lax.scan(advance, (zeroes, unity_ones), (values, pole), reverse=reverse)]
    dynamic_update_slice x2048 -> x0, other arithmetic: 41 us -> none  [local_pass(): lax.scan(advance, (zeroes, unity_ones), (values, pole), reverse=reverse)]
  transfers between devices with their start and end apart: 4 -> 0, of which waited for: 3 -> 0; matrix products, arithmetic and copies ran while one was open for 0% -> 0% of each run, Pallas kernels for 0% -> 0%
where the time goes in v1:
time: 71.9 us; the launch traced here: 71.6 us
  blocking collectives  64.1 us (89%)
  Pallas kernels  6.47 us (9%)
  other arithmetic  1 us (1%)
    all_to_all x2, blocking collectives, states(): chunks = lax.all_to_all(chunks, axis, 0, 0, tiled=True)  42 us
    all_to_all x2, blocking collectives, states(): return lax.all_to_all(entering, axis, 0, 0, tiled=True)  22.1 us
    pallas_call x5, Pallas kernels, call(): pl.pallas_call(kernel, out_shape=out_shape, scratch_shapes=scratch, compi...  6.47 us

profile of v1, /device:TPU:1, one launch (start us, length us, event | category | flops | bytes accessed | tf_op | source)
XLA Modules:
  0.0 71.6 jit_solution(11959114202854494698)
XLA Ops:
  0.0 1.0 %pad_maximum_fusion.arguments_ref = f32[520,128]{1,0:T(8,128)S(1)} fusion(f32[4,128]{1,0:T(4,128)} %param.5, f32[4,128]{1,0:T(4,128)} %param.4, f32[512,128]{1,0:T(8,128)} %bitcast.2), kind=kLoop, calls=%fused_computation | loop fusion | flops 133120 | bytes 532480 | tf_op jit(solution)/shard_map/concatenate | solution.py:445
  1.0 1.5 %shard_map.37 = (f32[512,128]{1,0:T(8,128)S(1)}, f32[4,128]{1,0:T(4,128)S(1)}, f32[520,128]{1,0:T(8,128)S(1)}, f32[520,128]{1,0:T(8,128)S(1)}, f32[37,8,128]{2,1,0:T(8,128)S(1)}, /*index=5*/f32[32,8,128]{2,1,0:T(8,128)S(1)}) custom-call(f32[520,128]{1,0:T(8,128)S(1)} %pad_maximum_fusion.arguments_ref), custom_call_target="tpu_custom_call" | custom-call | tf_op jit(solution)/shard_map/pallas_call | solution.py:424
  2.5 19.5 %all_to_all.20.blocks_ref = f32[32,8,128]{2,1,0:T(8,128)S(1)} all-to-all(f32[32,8,128]{2,1,0:T(8,128)S(1)} %get-tuple-element.20), channel_id=1, replica_groups=mesh['gx'=32,'gy'=16] {'gx'}, dimensions={0} | all-to-all | bytes 262144 | tf_op jit(solution)/shard_map/all_to_all | solution.py:430
  21.9 0.8 %shard_map.38 = f32[32,2,128]{2,1,0:T(2,128)S(1)} custom-call(f32[32,8,128]{2,1,0:T(8,128)S(1)} %all_to_all.20.blocks_ref), custom_call_target="tpu_custom_call" | custom-call | tf_op jit(solution)/shard_map/pallas_call | solution.py:424
  22.7 12.3 %all_to_all.21.state_ref = f32[32,2,128]{2,1,0:T(2,128)S(1)} all-to-all(f32[32,2,128]{2,1,0:T(2,128)S(1)} %shard_map.38), channel_id=1, replica_groups=mesh['gx'=32,'gy'=16] {'gx'}, dimensions={0} | all-to-all | bytes 65536 | tf_op jit(solution)/shard_map/all_to_all | solution.py:433
  35.0 2.1 %shard_map.39 = (f32[520,128]{1,0:T(8,128)S(1)}, f32[520,128]{1,0:T(8,128)S(1)}, f32[37,8,128]{2,1,0:T(8,128)S(1)}, f32[16,16,128]{2,1,0:T(8,128)S(1)}) custom-call(f32[512,128]{1,0:T(8,128)S(1)} %get-tuple-element.15.vt_ref, f32[4,128]{1,0:T(4,128)S(1)} %get-tuple-element.16.reach_ref, f32[520,128]{1,0:T(8,128)S(1)} %get-tuple-element.17.source_ref, ...), custom_call_target="tpu_custom_call" | custom-call | tf_op jit(solution)/shard_map/pallas_call | solution.py:424
  37.2 22.6 %all_to_all.22.blocks_ref = f32[16,16,128]{2,1,0:T(8,128)S(1)} all-to-all(f32[16,16,128]{2,1,0:T(8,128)S(1)} %get-tuple-element.24), channel_id=1, replica_groups=mesh['gx'=32,'gy'=16] {'gy'}, dimensions={0} | all-to-all | bytes 262144 | tf_op jit(solution)/shard_map/all_to_all | solution.py:430
  59.7 0.6 shard_map.40
  60.3 9.8 %all_to_all.23.state_ref = f32[16,4,128]{2,1,0:T(4,128)S(1)} all-to-all(f32[16,4,128]{2,1,0:T(4,128)S(1)} %shard_map.40), channel_id=1, replica_groups=mesh['gx'=32,'gy'=16] {'gy'}, dimensions={0} | all-to-all | bytes 65536 | tf_op jit(solution)/shard_map/all_to_all | solution.py:433
  70.1 1.5 %shard_map.41 = f32[512,128]{1,0:T(8,128)} custom-call(f32[520,128]{1,0:T(8,128)S(1)} %get-tuple-element.21.t_ref, f32[520,128]{1,0:T(8,128)S(1)} %get-tuple-element.22.d_ref, f32[37,8,128]{2,1,0:T(8,128)S(1)} %get-tuple-element.23.half_ref, f32[16,4,128]{2,1,0:T(4,128)S(1)} %all_to_all.23.state_ref), custom_call_target="tpu_custom_call" | custom-call | tf_op jit(solution)/shard_map/pallas_call | solution.py:424

commit v2 on v1

--- a/solution.py
+++ b/solution.py
@@ -113,7 +113,7 @@
     return p, [1.0 - x for x in p]
 
 
-STEPS, UNROLL = 64, 8
+STEPS, UNROLL = 64, 16
 PITCH = 65
 padded = (8 * PITCH, 128)
 
@@ -238,6 +238,14 @@
         pair_ref[pl.ds((37 + n) * APART, 4, stride=2), :] = value
     for n in range(44, SLOTS):
         pair_ref[n * APART : n * APART + 8, :] = jnp.zeros((8, 128), jnp.float32)
+    if chunks_ref.shape[1] == SLOTS:
+        row = lax.broadcasted_iota(jnp.int32, (8, 128), 0)
+        for z in range(4):
+            for n in range(0, SLOTS, 8):
+                x = pair_ref[pl.ds(n * APART + 2 * z, 8, stride=APART), :]
+                for at in range(z, chunks_ref.shape[0], 4):
+                    chunks_ref[at, n : n + 8, :] = x if n != 40 else jnp.where(row == 4, float(at // 4), x)
+        return
     per_plane = chunks_ref.shape[0] // 4
     groups = per_plane
     for z in range(4):
@@ -250,16 +258,19 @@
 
 def finish(v_ref, half_ref, state_ref, d_ref, c_ref, out_ref, wide_ref):
     groups = state_ref.shape[0] // 4
-    count = 8 // groups
     for z in range(4):
         chunks = slice(z * groups, (z + 1) * groups)
-        x = swap(jnp.concatenate([state_ref[chunks, a, :] for a in range(count)], axis=0), groups)
+        if groups == 1:
+            x, ends = state_ref[z, 0:8, :], state_ref[z, 8:16, :]
+        else:
+            count = 8 // groups
+            x = swap(jnp.concatenate([state_ref[chunks, a, :] for a in range(count)], axis=0), groups)
+            ends = swap(jnp.concatenate([state_ref[chunks, count, :]] * count, axis=0), groups)
         wide_ref[pl.ds(2 * z, 8, stride=APART), :] = x
         wide_ref[pl.ds(2 * z + 1, 8, stride=APART), :] = x
-        x = swap(jnp.concatenate([state_ref[chunks, count, :]] * count, axis=0), groups)
         first, last = 2 * z * PITCH, (2 * z + 1) * PITCH + STEPS - 1
-        d_ref[first : first + 1, :] = x[0:1]
-        d_ref[last : last + 1, :] = x[1:2]
+        d_ref[first : first + 1, :] = ends[0:1]
+        d_ref[last : last + 1, :] = ends[1:2]
     f = [wide_ref[k * APART : k * APART + 8, :] for k in range(4)]
     b = [wide_ref[k * APART : k * APART + 8, :] for k in range(4, 8)]
     block = unpack(lambda n: half_ref[n])
@@ -415,6 +426,54 @@
         state_ref[:, r, :] = jnp.zeros((count, 128), jnp.float32)
 
 
+def plane_scan(blocks_ref, state_ref, map_ref, f_ref, b_ref):
+    count = blocks_ref.shape[0]
+    row = lax.broadcasted_iota(jnp.int32, (count, 128), 0)
+    value = lambda n: blocks_ref[:, n, :]
+    v = [value(37 + n) for n in range(4)]
+    below = jnp.where(row == 0, 0.0, pltpu.roll(v[3], 1, 0))
+    above = jnp.where(row == count - 1, 0.0, pltpu.roll(v[0], count - 1, 0))
+    inverse = -1.0 / value(43)
+    for n, gradient in enumerate((0.5 * (v[1] - below), 0.5 * (above - v[2]))):
+        map_ref[37 + n] = jnp.exp((1.0 + edge_slope * jnp.abs(gradient)) * inverse)
+    for start in range(0, count, 8):
+        some = slice(start, start + 8)
+        block = unpack(lambda n: blocks_ref[some, n, :])
+        block = with_ends(block, map_ref[37, some, :], map_ref[38, some, :], blocks_ref[some, 41, :], blocks_ref[some, 42, :])
+        for n, x in enumerate(pack(block)):
+            map_ref[n, some, :] = x
+
+    def block_at(m):
+        return unpack(lambda n: map_ref[n, m : m + 1, :])
+
+    f = [jnp.zeros((1, 128), jnp.float32)] * 4
+    for m in range(count):
+        for k in range(4):
+            f_ref[k, m : m + 1, :] = f[k]
+        f = forward_out(block_at(m), f)
+    b = [jnp.zeros((1, 128), jnp.float32)] * 4
+    for m in reversed(range(count)):
+        for k in range(4):
+            b_ref[k, m : m + 1, :] = b[k]
+        b = backward_out(block_at(m), [f_ref[k, m : m + 1, :] for k in range(4)], b)
+
+    here = jnp.broadcast_to(blocks_ref[0, 44:45, :], (4, 128))
+
+    def mine(at):
+        x = at(0)
+        for g in range(1, count // 4):
+            x = jnp.where(here == float(g), at(g), x)
+        return x
+
+    for k in range(4):
+        state_ref[:, k, :] = mine(lambda g: f_ref[k, 4 * g : 4 * g + 4, :])
+        state_ref[:, 4 + k, :] = mine(lambda g: b_ref[k, 4 * g : 4 * g + 4, :])
+    for n in range(2):
+        state_ref[:, 8 + n, :] = mine(lambda g: map_ref[37 + n, 4 * g : 4 * g + 4, :])
+    for n in range(10, 16):
+        state_ref[:, n, :] = jnp.zeros((4, 128), jnp.float32)
+
+
 f32 = lambda *shape: jax.ShapeDtypeStruct(shape, jnp.float32)
 vmem = lambda *shape: pltpu.VMEM(shape, jnp.float32)
 plane = (512, 128)
@@ -433,10 +492,18 @@
     return lax.all_to_all(entering, axis, 0, 0, tiled=True)
 
 
+def states_by_planes(chunks, axis):
+    size = lax.axis_size(axis)
+    blocks = lax.all_to_all(chunks, axis, 0, 0, tiled=True)
+    entering = call(plane_scan, f32(4, 16, 128), [vmem(39, size, 128), vmem(4, size, 128), vmem(4, size, 128)], blocks)
+    fours = [[4 * g + i for i in range(4)] for g in range(size // 4)]
+    return lax.all_to_all(entering, axis, 0, 0, axis_index_groups=fours, tiled=True)
+
+
 def per_device(intensity, reach_along_x, reach_along_y):
     def maps(axis):
         size = lax.axis_size(axis)
-        return [f32(*padded), f32(37, 8, 128), f32(size, 256 // size, 128)]
+        return [f32(*padded), f32(37, 8, 128), f32(size, SLOTS if axis == "gy" else 256 // size, 128)]
 
     work = [vmem(SLOTS * APART, 128)]
     ending = [vmem(*padded), vmem(STEPS, 8, 128), vmem(*padded), vmem(8 * APART, 128)]
@@ -448,7 +515,7 @@
     t, dy, y_half, y_chunks = call(
         x_second_y_first, [f32(*padded)] + maps("gy"), ending + work, vt, y_reach, source, dx, x_half, x_states
     )
-    y_states = states(y_chunks, "gy")
+    y_states = states_by_planes(y_chunks, "gy")
     out = call(y_second, f32(*plane), ending, t, dy, y_half, y_states)
     return out.reshape(4, 128, 128)
 

time: 71.9 us -> 71.6 us (level)
    all_to_all x0 -> x2, blocking collectives: none -> 32.7 us  [the longest x1 27.9 us: states_by_planes(): blocks = lax.all_to_all(chunks, axis, 0, 0, tiled=True)]
    all_to_all x2 -> x1, blocking collectives: 42 us -> 19.5 us  [states(): chunks = lax.all_to_all(chunks, axis, 0, 0, tiled=True)]
    all_to_all x2 -> x1, blocking collectives: 22.1 us -> 12.3 us  [states(): return lax.all_to_all(entering, axis, 0, 0, tiled=True)]
where the time goes in v2:
time: 71.6 us; the launch traced here: 71.3 us
  blocking collectives  64.5 us (90%)
  Pallas kernels  5.84 us (8%)
  other arithmetic  1 us (1%)
    all_to_all x1, blocking collectives, states_by_planes(): blocks = lax.all_to_all(chunks, axis, 0, 0, tiled=True)  27.9 us
    all_to_all x1, blocking collectives, states(): chunks = lax.all_to_all(chunks, axis, 0, 0, tiled=True)  19.5 us
    all_to_all x1, blocking collectives, states(): return lax.all_to_all(entering, axis, 0, 0, tiled=True)  12.3 us
    pallas_call x5, Pallas kernels, call(): pl.pallas_call(kernel, out_shape=out_shape, scratch_shapes=scratch, compi...  5.84 us
    all_to_all x1, blocking collectives, states_by_planes(): lax.all_to_all(entering, axis, 0, 0, axis_index_groups=fours, tiled=True)  4.76 us

profile of v2, /device:TPU:1, one launch (start us, length us, event | category | flops | bytes accessed | tf_op | source)
XLA Modules:
  0.0 71.3 jit_solution(1981185796921088300)
XLA Ops:
  0.0 1.0 %pad_maximum_fusion.arguments_ref = f32[520,128]{1,0:T(8,128)S(1)} fusion(f32[4,128]{1,0:T(4,128)} %param.5, f32[4,128]{1,0:T(4,128)} %param.4, f32[512,128]{1,0:T(8,128)} %bitcast.2), kind=kLoop, calls=%fused_computation | loop fusion | flops 133120 | bytes 532480 | tf_op jit(solution)/shard_map/concatenate | solution.py:512
  1.0 1.5 %shard_map.37 = (f32[512,128]{1,0:T(8,128)S(1)}, f32[4,128]{1,0:T(4,128)S(1)}, f32[520,128]{1,0:T(8,128)S(1)}, f32[520,128]{1,0:T(8,128)S(1)}, f32[37,8,128]{2,1,0:T(8,128)S(1)}, /*index=5*/f32[32,8,128]{2,1,0:T(8,128)S(1)}) custom-call(f32[520,128]{1,0:T(8,128)S(1)} %pad_maximum_fusion.arguments_ref), custom_call_target="tpu_custom_call" | custom-call | tf_op jit(solution)/shard_map/pallas_call | solution.py:483
  2.5 19.5 %all_to_all.20.blocks_ref = f32[32,8,128]{2,1,0:T(8,128)S(1)} all-to-all(f32[32,8,128]{2,1,0:T(8,128)S(1)} %get-tuple-element.20), channel_id=1, replica_groups=mesh['gx'=32,'gy'=16] {'gx'}, dimensions={0} | all-to-all | bytes 262144 | tf_op jit(solution)/shard_map/all_to_all | solution.py:489
  21.9 0.8 %shard_map.38 = f32[32,2,128]{2,1,0:T(2,128)S(1)} custom-call(f32[32,8,128]{2,1,0:T(8,128)S(1)} %all_to_all.20.blocks_ref), custom_call_target="tpu_custom_call" | custom-call | tf_op jit(solution)/shard_map/pallas_call | solution.py:483
  22.7 12.3 %all_to_all.21.state_ref = f32[32,2,128]{2,1,0:T(2,128)S(1)} all-to-all(f32[32,2,128]{2,1,0:T(2,128)S(1)} %shard_map.38), channel_id=1, replica_groups=mesh['gx'=32,'gy'=16] {'gx'}, dimensions={0} | all-to-all | bytes 65536 | tf_op jit(solution)/shard_map/all_to_all | solution.py:492
  35.0 1.8 %shard_map.39 = (f32[520,128]{1,0:T(8,128)S(1)}, f32[520,128]{1,0:T(8,128)S(1)}, f32[37,8,128]{2,1,0:T(8,128)S(1)}, f32[16,48,128]{2,1,0:T(8,128)S(1)}) custom-call(f32[512,128]{1,0:T(8,128)S(1)} %get-tuple-element.15.vt_ref, f32[4,128]{1,0:T(4,128)S(1)} %get-tuple-element.16.reach_ref, f32[520,128]{1,0:T(8,128)S(1)} %get-tuple-element.17.source_ref, ...), custom_call_target="tpu_custom_call" | custom-call | tf_op jit(solution)/shard_map/pallas_call | solution.py:483
  36.8 27.9 %all_to_all.22.blocks_ref = f32[16,48,128]{2,1,0:T(8,128)S(1)} all-to-all(f32[16,48,128]{2,1,0:T(8,128)S(1)} %get-tuple-element.24), channel_id=1, replica_groups=mesh['gx'=32,'gy'=16] {'gy'}, dimensions={0} | all-to-all | bytes 786432 | tf_op jit(solution)/shard_map/all_to_all | solution.py:497
  64.8 0.5 shard_map.40
  65.3 4.8 %all_to_all.23.state_ref = f32[4,16,128]{2,1,0:T(8,128)S(1)} all-to-all(f32[4,16,128]{2,1,0:T(8,128)S(1)} %shard_map.40), channel_id=1, replica_groups={{0,1,2,3},{4,5,6,7},{8,9,10,11},{12,13,14,15},{16,17,18,19},{20,21,22,2..., dimensions={0} | all-to-all | bytes 65536 | tf_op jit(solution)/shard_map/all_to_all | solution.py:500
  70.0 1.3 %shard_map.41 = f32[512,128]{1,0:T(8,128)} custom-call(f32[520,128]{1,0:T(8,128)S(1)} %get-tuple-element.21.t_ref, f32[520,128]{1,0:T(8,128)S(1)} %get-tuple-element.22.d_ref, f32[37,8,128]{2,1,0:T(8,128)S(1)} %get-tuple-element.23.half_ref, f32[4,16,128]{2,1,0:T(8,128)S(1)} %all_to_all.23.state_ref), custom_call_target="tpu_custom_call" | custom-call | tf_op jit(solution)/shard_map/pallas_call | solution.py:483

commit v3 on v2

--- a/solution.py
+++ b/solution.py
@@ -238,13 +238,12 @@
         pair_ref[pl.ds((37 + n) * APART, 4, stride=2), :] = value
     for n in range(44, SLOTS):
         pair_ref[n * APART : n * APART + 8, :] = jnp.zeros((8, 128), jnp.float32)
-    if chunks_ref.shape[1] == SLOTS:
-        row = lax.broadcasted_iota(jnp.int32, (8, 128), 0)
+    if chunks_ref.shape[2] == 4:
         for z in range(4):
-            for n in range(0, SLOTS, 8):
-                x = pair_ref[pl.ds(n * APART + 2 * z, 8, stride=APART), :]
+            for n in range(0, 44, 4):
+                x = pair_ref[pl.ds(n * APART + 2 * z, 4, stride=APART), :]
                 for at in range(z, chunks_ref.shape[0], 4):
-                    chunks_ref[at, n : n + 8, :] = x if n != 40 else jnp.where(row == 4, float(at // 4), x)
+                    chunks_ref[at, n // 4] = x
         return
     per_plane = chunks_ref.shape[0] // 4
     groups = per_plane
@@ -253,7 +252,8 @@
         for n in range(0, SLOTS, 8):
             x = swap(pair_ref[pl.ds(n * APART + 2 * z, 8, stride=APART), :], groups)
             for a in range(8 // groups):
-                chunks_ref[chunks, n // groups + a, :] = x[a * groups : (a + 1) * groups]
+                r = n // groups + a
+                chunks_ref[chunks, r // 2, r % 2, :] = x[a * groups : (a + 1) * groups]
 
 
 def finish(v_ref, half_ref, state_ref, d_ref, c_ref, out_ref, wide_ref):
@@ -362,7 +362,7 @@
         return pltpu.roll(x, by, 1) if by else x
 
     def value(n):
-        parts = [moved(blocks_ref[8 * g : 8 * g + 8, n // groups, :], g - n % groups) for g in range(eights)]
+        parts = [moved(blocks_ref[8 * g : 8 * g + 8, n // groups // 2, n // groups % 2, :], g - n % groups) for g in range(eights)]
         x = parts[0]
         for g in range(1, eights):
             x = jnp.where(group == g, parts[g], x)
@@ -426,10 +426,10 @@
         state_ref[:, r, :] = jnp.zeros((count, 128), jnp.float32)
 
 
-def plane_scan(blocks_ref, state_ref, map_ref, f_ref, b_ref):
+def plane_scan(here_ref, blocks_ref, state_ref, map_ref, f_ref, b_ref):
     count = blocks_ref.shape[0]
     row = lax.broadcasted_iota(jnp.int32, (count, 128), 0)
-    value = lambda n: blocks_ref[:, n, :]
+    value = lambda n, some=slice(None): blocks_ref[some, n // 4, n % 4, :]
     v = [value(37 + n) for n in range(4)]
     below = jnp.where(row == 0, 0.0, pltpu.roll(v[3], 1, 0))
     above = jnp.where(row == count - 1, 0.0, pltpu.roll(v[0], count - 1, 0))
@@ -438,8 +438,8 @@
         map_ref[37 + n] = jnp.exp((1.0 + edge_slope * jnp.abs(gradient)) * inverse)
     for start in range(0, count, 8):
         some = slice(start, start + 8)
-        block = unpack(lambda n: blocks_ref[some, n, :])
-        block = with_ends(block, map_ref[37, some, :], map_ref[38, some, :], blocks_ref[some, 41, :], blocks_ref[some, 42, :])
+        block = unpack(lambda n: value(n, some))
+        block = with_ends(block, map_ref[37, some, :], map_ref[38, some, :], value(41, some), value(42, some))
         for n, x in enumerate(pack(block)):
             map_ref[n, some, :] = x
 
@@ -457,12 +457,12 @@
             b_ref[k, m : m + 1, :] = b[k]
         b = backward_out(block_at(m), [f_ref[k, m : m + 1, :] for k in range(4)], b)
 
-    here = jnp.broadcast_to(blocks_ref[0, 44:45, :], (4, 128))
+    here = here_ref[...]
 
     def mine(at):
         x = at(0)
         for g in range(1, count // 4):
-            x = jnp.where(here == float(g), at(g), x)
+            x = jnp.where(here == g, at(g), x)
         return x
 
     for k in range(4):
@@ -492,10 +492,10 @@
     return lax.all_to_all(entering, axis, 0, 0, tiled=True)
 
 
-def states_by_planes(chunks, axis):
+def states_by_planes(chunks, axis, group):
     size = lax.axis_size(axis)
     blocks = lax.all_to_all(chunks, axis, 0, 0, tiled=True)
-    entering = call(plane_scan, f32(4, 16, 128), [vmem(39, size, 128), vmem(4, size, 128), vmem(4, size, 128)], blocks)
+    entering = call(plane_scan, f32(4, 16, 128), [vmem(39, size, 128), vmem(4, size, 128), vmem(4, size, 128)], group, blocks)
     fours = [[4 * g + i for i in range(4)] for g in range(size // 4)]
     return lax.all_to_all(entering, axis, 0, 0, axis_index_groups=fours, tiled=True)
 
@@ -503,7 +503,9 @@
 def per_device(intensity, reach_along_x, reach_along_y):
     def maps(axis):
         size = lax.axis_size(axis)
-        return [f32(*padded), f32(37, 8, 128), f32(size, SLOTS if axis == "gy" else 256 // size, 128)]
+        return [f32(*padded), f32(37, 8, 128), f32(size, 11, 4, 128) if axis == "gy" else f32(size, SLOTS * 2 // size, 2, 128)]
+
+    group = jnp.full((4, 128), lax.shift_right_logical(lax.axis_index("gy"), 2), jnp.int32)
 
     work = [vmem(SLOTS * APART, 128)]
     ending = [vmem(*padded), vmem(STEPS, 8, 128), vmem(*padded), vmem(8 * APART, 128)]
@@ -515,7 +517,7 @@
     t, dy, y_half, y_chunks = call(
         x_second_y_first, [f32(*padded)] + maps("gy"), ending + work, vt, y_reach, source, dx, x_half, x_states
     )
-    y_states = states_by_planes(y_chunks, "gy")
+    y_states = states_by_planes(y_chunks, "gy", group)
     out = call(y_second, f32(*plane), ending, t, dy, y_half, y_states)
     return out.reshape(4, 128, 128)
 

time: 71.6 us -> 71.6 us (level)
  blocking collectives: 64.5 us -> 36.2 us
  waiting for transfers between devices: 0 us -> 13.8 us
  starting transfers between devices: 0 us -> 13.6 us
  Pallas kernels: 5.84 us -> 6.59 us
    all_to_all x1 -> x0, blocking collectives: 27.9 us -> none  [states_by_planes(): blocks = lax.all_to_all(chunks, axis, 0, 0, tiled=True)]
    all_to_all x0 -> x1, waiting for transfers between devices: none -> 13.8 us  [states_by_planes(): blocks = lax.all_to_all(chunks, axis, 0, 0, tiled=True)]
    all_to_all x0 -> x1, starting transfers between devices: none -> 13.6 us  [states_by_planes(): blocks = lax.all_to_all(chunks, axis, 0, 0, tiled=True)]
    pallas_call x5, Pallas kernels: 5.84 us -> 6.59 us  [call(): pl.pallas_call(kernel, out_shape=out_shape, scratch_shapes=scratch, compi...]
  transfers between devices with their start and end apart: 0 -> 1, of which waited for: 0 -> 1; matrix products, arithmetic and copies ran while one was open for 0% -> 0% of each run, Pallas kernels for 0% -> 0%
where the time goes in v3:
time: 71.6 us; the launch traced here: 71.3 us
  blocking collectives  36.2 us (51%)
  waiting for transfers between devices  13.8 us (19%)
  starting transfers between devices  13.6 us (19%)
  Pallas kernels  6.59 us (9%)
  other arithmetic  1 us (1%)
    all_to_all x1, blocking collectives, states(): chunks = lax.all_to_all(chunks, axis, 0, 0, tiled=True)  19.3 us
    all_to_all x1, waiting for transfers between devices, states_by_planes(): blocks = lax.all_to_all(chunks, axis, 0, 0, tiled=True)  13.8 us
    all_to_all x1, starting transfers between devices, states_by_planes(): blocks = lax.all_to_all(chunks, axis, 0, 0, tiled=True)  13.6 us
    all_to_all x1, blocking collectives, states(): return lax.all_to_all(entering, axis, 0, 0, tiled=True)  12.1 us
    pallas_call x5, Pallas kernels, call(): pl.pallas_call(kernel, out_shape=out_shape, scratch_shapes=scratch, compi...  6.59 us
    all_to_all x1, blocking collectives, states_by_planes(): lax.all_to_all(entering, axis, 0, 0, axis_index_groups=fours, tiled=True)  4.85 us
  transfers between devices with their start and end apart: 1, of which 1 were waited for; matrix products, arithmetic and copies ran while one was open for 0% of the time, Pallas kernels for 0%

profile of v3, /device:TPU:1, one launch (start us, length us, event | category | flops | bytes accessed | tf_op | source)
XLA Modules:
  0.0 71.3 jit_solution(7921271554620159441)
XLA Ops:
  0.0 1.0 %pad_maximum_fusion.arguments_ref = f32[520,128]{1,0:T(8,128)S(1)} fusion(f32[4,128]{1,0:T(4,128)} %param.5, f32[4,128]{1,0:T(4,128)} %param.4, f32[512,128]{1,0:T(8,128)} %bitcast.2), kind=kLoop, calls=%fused_computation | loop fusion | flops 133120 | bytes 532480 | tf_op jit(solution)/shard_map/concatenate | solution.py:514
  1.0 1.5 %shard_map.37 = (f32[512,128]{1,0:T(8,128)S(1)}, f32[4,128]{1,0:T(4,128)S(1)}, f32[520,128]{1,0:T(8,128)S(1)}, f32[520,128]{1,0:T(8,128)S(1)}, f32[37,8,128]{2,1,0:T(8,128)S(1)}, /*index=5*/f32[32,3,2,128]{3,2,1,0:T(2,128)S(1)}) custom-call(f32[520,128]{1,0:T(8,128)S(1)} %pad_maximum_fusion.arguments_ref), custom_call_target="tpu_custom_call" | custom-call | tf_op jit(solution)/shard_map/pallas_call | solution.py:483
  2.5 19.3 %all_to_all.20.blocks_ref = f32[32,3,2,128]{3,2,1,0:T(2,128)S(1)} all-to-all(f32[32,3,2,128]{3,2,1,0:T(2,128)S(1)} %get-tuple-element.20), channel_id=1, replica_groups=mesh['gx'=32,'gy'=16] {'gx'}, dimensions={0} | all-to-all | bytes 196608 | tf_op jit(solution)/shard_map/all_to_all | solution.py:489
  21.8 0.8 %shard_map.38 = f32[32,2,128]{2,1,0:T(2,128)S(1)} custom-call(f32[32,3,2,128]{3,2,1,0:T(2,128)S(1)} %all_to_all.20.blocks_ref), custom_call_target="tpu_custom_call" | custom-call | tf_op jit(solution)/shard_map/pallas_call | solution.py:483
  22.6 12.1 %all_to_all.21.state_ref = f32[32,2,128]{2,1,0:T(2,128)S(1)} all-to-all(f32[32,2,128]{2,1,0:T(2,128)S(1)} %shard_map.38), channel_id=1, replica_groups=mesh['gx'=32,'gy'=16] {'gx'}, dimensions={0} | all-to-all | bytes 65536 | tf_op jit(solution)/shard_map/all_to_all | solution.py:492
  34.6 2.6 %shard_map.39 = (f32[520,128]{1,0:T(8,128)S(1)}, f32[520,128]{1,0:T(8,128)S(1)}, f32[37,8,128]{2,1,0:T(8,128)S(1)}, f32[16,11,4,128]{3,2,1,0:T(4,128)}) custom-call(f32[512,128]{1,0:T(8,128)S(1)} %get-tuple-element.15.vt_ref, f32[4,128]{1,0:T(4,128)S(1)} %get-tuple-element.16.reach_ref, f32[520,128]{1,0:T(8,128)S(1)} %get-tuple-element.17.source_ref, ...), custom_call_target="tpu_custom_call" | custom-call | tf_op jit(solution)/shard_map/pallas_call | solution.py:483
  37.2 13.6 %all-to-all-start.2 = ((f32[16,11,4,128]{3,2,1,0:T(4,128)}), f32[16,11,4,128]{3,2,1,0:T(4,128)S(1)}, u32[]{:S(2)}, u32[]{:S(2)}) async-start(f32[16,11,4,128]{3,2,1,0:T(4,128)} %get-tuple-element.24), calls=%async_computation.2 | async-start | bytes 720896 | tf_op jit(solution)/shard_map/all_to_all | solution.py:497
  50.8 13.8 %all-to-all-done.2.blocks_ref = f32[16,11,4,128]{3,2,1,0:T(4,128)S(1)} async-done(((f32[16,11,4,128]{3,2,1,0:T(4,128)}), f32[16,11,4,128]{3,2,1,0:T(4,128)S(1)}, u32[]{:S(2)}, u32[]{:S(2)}) %all-to-all-start.2) | async-done | bytes 360480 | tf_op jit(solution)/shard_map/all_to_all | solution.py:497
  64.7 0.5 shard_map.40
  65.2 4.8 %all_to_all.22.state_ref = f32[4,16,128]{2,1,0:T(8,128)S(1)} all-to-all(f32[4,16,128]{2,1,0:T(8,128)S(1)} %shard_map.40), channel_id=1, replica_groups={{0,1,2,3},{4,5,6,7},{8,9,10,11},{12,13,14,15},{16,17,18,19},{20,21,22,2..., dimensions={0} | all-to-all | bytes 65536 | tf_op jit(solution)/shard_map/all_to_all | solution.py:500
  70.0 1.3 %shard_map.41 = f32[512,128]{1,0:T(8,128)} custom-call(f32[520,128]{1,0:T(8,128)S(1)} %get-tuple-element.21.t_ref, f32[520,128]{1,0:T(8,128)S(1)} %get-tuple-element.22.d_ref, f32[37,8,128]{2,1,0:T(8,128)S(1)} %get-tuple-element.23.half_ref, f32[4,16,128]{2,1,0:T(8,128)S(1)} %all_to_all.22.state_ref), custom_call_target="tpu_custom_call" | custom-call | tf_op jit(solution)/shard_map/pallas_call | solution.py:483
  (1 shorter events, 0.0 us)
Async XLA Ops:
  37.2 27.4 %all-to-all-start.2 = ((f32[16,11,4,128]{3,2,1,0:T(4,128)}), f32[16,11,4,128]{3,2,1,0:T(4,128)S(1)}, u32[]{:S(2)}, u32[]{:S(2)}) async-start(f32[16,11,4,128]{3,2,1,0:T(4,128)} %get-tuple-element.24), calls=%async_computation.2 | async-start | bytes 720896 | tf_op jit(solution)/shard_map/all_to_all | solution.py:497

commit v4 on v3

--- a/solution.py
+++ b/solution.py
@@ -300,10 +300,11 @@
     loop(backward, b, reverse=True)
 
 
-def x_first(arguments_ref, vt_ref, y_reach_ref, source_ref, d_ref, half_ref, chunks_ref, reach_ref, pair_ref):
+def x_first(arguments_ref, here_ref, vt_ref, y_reach_ref, group_ref, source_ref, d_ref, half_ref, chunks_ref, reach_ref, pair_ref):
     for z, here in enumerate(planes()):
         vt_ref[here, :] = arguments_ref[here, :].T
         spread(source_ref, z, arguments_ref[here, :])
+    group_ref[...] = here_ref[...]
     reach_ref[...] = arguments_ref[512:516, :]
     y_reach_ref[...] = arguments_ref[516:520, :]
     summarise(arguments_ref, source_ref, reach_ref, d_ref, half_ref, chunks_ref, pair_ref)
@@ -509,9 +510,9 @@
 
     work = [vmem(SLOTS * APART, 128)]
     ending = [vmem(*padded), vmem(STEPS, 8, 128), vmem(*padded), vmem(8 * APART, 128)]
-    vt, y_reach, source, dx, x_half, x_chunks = call(
-        x_first, [f32(*plane), f32(4, 128), f32(*padded)] + maps("gx"), [vmem(4, 128)] + work,
-        jnp.concatenate([intensity.reshape(plane), reach_along_x, reach_along_y]),
+    vt, y_reach, group, source, dx, x_half, x_chunks = call(
+        x_first, [f32(*plane), f32(4, 128), jax.ShapeDtypeStruct((4, 128), jnp.int32), f32(*padded)] + maps("gx"), [vmem(4, 128)] + work,
+        jnp.concatenate([intensity.reshape(plane), reach_along_x, reach_along_y]), group,
     )
     x_states = states(x_chunks, "gx")
     t, dy, y_half, y_chunks = call(

time: 71.6 us -> 71.3 us (level)
  blocking collectives: 36.2 us -> 63.5 us
  waiting for transfers between devices: 13.8 us -> 0 us
  starting transfers between devices: 13.6 us -> 0 us
  Pallas kernels: 6.59 us -> 5.86 us
    all_to_all x0 -> x1, blocking collectives: none -> 27.2 us  [states_by_planes(): blocks = lax.all_to_all(chunks, axis, 0, 0, tiled=True)]
    all_to_all x1 -> x0, waiting for transfers between devices: 13.8 us -> none  [states_by_planes(): blocks = lax.all_to_all(chunks, axis, 0, 0, tiled=True)]
    all_to_all x1 -> x0, starting transfers between devices: 13.6 us -> none  [states_by_planes(): blocks = lax.all_to_all(chunks, axis, 0, 0, tiled=True)]
    pallas_call x5, Pallas kernels: 6.59 us -> 5.86 us  [call(): pl.pallas_call(kernel, out_shape=out_shape, scratch_shapes=scratch, compi...]
  transfers between devices with their start and end apart: 1 -> 0, of which waited for: 1 -> 0; matrix products, arithmetic and copies ran while one was open for 0% -> 0% of each run, Pallas kernels for 0% -> 0%
where the time goes in v4:
time: 71.3 us; the launch traced here: 71 us
  blocking collectives  63.5 us (89%)
  Pallas kernels  5.86 us (8%)
  other arithmetic  0.97 us (1%)
    all_to_all x1, blocking collectives, states_by_planes(): blocks = lax.all_to_all(chunks, axis, 0, 0, tiled=True)  27.2 us
    all_to_all x1, blocking collectives, states(): chunks = lax.all_to_all(chunks, axis, 0, 0, tiled=True)  19.3 us
    all_to_all x1, blocking collectives, states(): return lax.all_to_all(entering, axis, 0, 0, tiled=True)  12.1 us
    pallas_call x5, Pallas kernels, call(): pl.pallas_call(kernel, out_shape=out_shape, scratch_shapes=scratch, compi...  5.86 us
    all_to_all x1, blocking collectives, states_by_planes(): lax.all_to_all(entering, axis, 0, 0, axis_index_groups=fours, tiled=True)  4.85 us

profile of v4, /device:TPU:1, one launch (start us, length us, event | category | flops | bytes accessed | tf_op | source)
XLA Modules:
  0.0 71.0 jit_solution(14459552530776771845)
XLA Ops:
  0.0 0.0 copy-start.1
  0.0 0.0 copy-start
  0.0 0.7 copy-done.1
  0.7 0.0 copy-done
  0.7 1.0 %pad_maximum_fusion.arguments_ref = f32[520,128]{1,0:T(8,128)S(1)} fusion(f32[4,128]{1,0:T(4,128)S(1)} %copy-done, f32[4,128]{1,0:T(4,128)S(1)} %copy-done.1, f32[512,128]{1,0:T(8,128)} %bitcast.2), kind=kLoop, calls=%fused_computation | loop fusion | flops 133120 | bytes 532480 | tf_op jit(solution)/shard_map/concatenate | solution.py:515
  1.7 1.5 %shard_map.37 = (f32[512,128]{1,0:T(8,128)S(1)}, f32[4,128]{1,0:T(4,128)S(1)}, s32[4,128]{1,0:T(4,128)S(1)}, f32[520,128]{1,0:T(8,128)S(1)}, f32[520,128]{1,0:T(...) custom-call(f32[520,128]{1,0:T(8,128)S(1)} %pad_maximum_fusion.arguments_ref, ...), custom_call_target="tpu_custom_call" | custom-call | tf_op jit(solution)/shard_map/pallas_call | solution.py:484
  3.1 19.3 %all_to_all.20.blocks_ref = f32[32,3,2,128]{3,2,1,0:T(2,128)S(1)} all-to-all(f32[32,3,2,128]{3,2,1,0:T(2,128)S(1)} %get-tuple-element.21), channel_id=1, replica_groups=mesh['gx'=32,'gy'=16] {'gx'}, dimensions={0} | all-to-all | bytes 196608 | tf_op jit(solution)/shard_map/all_to_all | solution.py:490
  22.5 0.8 %shard_map.38 = f32[32,2,128]{2,1,0:T(2,128)S(1)} custom-call(f32[32,3,2,128]{3,2,1,0:T(2,128)S(1)} %all_to_all.20.blocks_ref), custom_call_target="tpu_custom_call" | custom-call | tf_op jit(solution)/shard_map/pallas_call | solution.py:484
  23.3 12.1 %all_to_all.21.state_ref = f32[32,2,128]{2,1,0:T(2,128)S(1)} all-to-all(f32[32,2,128]{2,1,0:T(2,128)S(1)} %shard_map.38), channel_id=1, replica_groups=mesh['gx'=32,'gy'=16] {'gx'}, dimensions={0} | all-to-all | bytes 65536 | tf_op jit(solution)/shard_map/all_to_all | solution.py:493
  35.3 1.8 %shard_map.39 = (f32[520,128]{1,0:T(8,128)S(1)}, f32[520,128]{1,0:T(8,128)S(1)}, f32[37,8,128]{2,1,0:T(8,128)S(1)}, f32[16,11,4,128]{3,2,1,0:T(4,128)S(1)}) custom-call(f32[512,128]{1,0:T(8,128)S(1)} %get-tuple-element.16.vt_ref, f32[4,128]{1,0:T(4,128)S(1)} %get-tuple-element.17.reach_ref, f32[520,128]{1,0:T(8,128)S(1)} %get-tuple-element.18.source_ref, ...), custom_call_target="tpu_custom_call" | custom-call | tf_op jit(solution)/shard_map/pallas_call | solution.py:484
  37.2 27.2 %all_to_all.22.blocks_ref = f32[16,11,4,128]{3,2,1,0:T(4,128)S(1)} all-to-all(f32[16,11,4,128]{3,2,1,0:T(4,128)S(1)} %get-tuple-element.26), channel_id=1, replica_groups=mesh['gx'=32,'gy'=16] {'gy'}, dimensions={0} | all-to-all | bytes 720896 | tf_op jit(solution)/shard_map/all_to_all | solution.py:498
  64.4 0.5 shard_map.40
  64.9 4.8 %all_to_all.23.state_ref = f32[4,16,128]{2,1,0:T(8,128)S(1)} all-to-all(f32[4,16,128]{2,1,0:T(8,128)S(1)} %shard_map.40), channel_id=1, replica_groups={{0,1,2,3},{4,5,6,7},{8,9,10,11},{12,13,14,15},{16,17,18,19},{20,21,22,2..., dimensions={0} | all-to-all | bytes 65536 | tf_op jit(solution)/shard_map/all_to_all | solution.py:501
  69.7 1.3 %shard_map.41 = f32[512,128]{1,0:T(8,128)} custom-call(f32[520,128]{1,0:T(8,128)S(1)} %get-tuple-element.22.t_ref, f32[520,128]{1,0:T(8,128)S(1)} %get-tuple-element.23.d_ref, f32[37,8,128]{2,1,0:T(8,128)S(1)} %get-tuple-element.24.half_ref, f32[4,16,128]{2,1,0:T(8,128)S(1)} %all_to_all.23.state_ref), custom_call_target="tpu_custom_call" | custom-call | tf_op jit(solution)/shard_map/pallas_call | solution.py:484
  (1 shorter events, 0.0 us)
Async XLA Ops:
  0.0 0.7 copy-start.1
  0.0 0.7 copy-start

commit v5 on v3

--- a/solution.py
+++ b/solution.py
@@ -239,11 +239,12 @@
     for n in range(44, SLOTS):
         pair_ref[n * APART : n * APART + 8, :] = jnp.zeros((8, 128), jnp.float32)
     if chunks_ref.shape[2] == 4:
+        row = lax.broadcasted_iota(jnp.int32, (4, 128), 0)
         for z in range(4):
             for n in range(0, 44, 4):
                 x = pair_ref[pl.ds(n * APART + 2 * z, 4, stride=APART), :]
                 for at in range(z, chunks_ref.shape[0], 4):
-                    chunks_ref[at, n // 4] = x
+                    chunks_ref[at, n // 4] = x if n != 40 else jnp.where(row == 3, float(at), x)
         return
     per_plane = chunks_ref.shape[0] // 4
     groups = per_plane
@@ -426,14 +427,18 @@
         state_ref[:, r, :] = jnp.zeros((count, 128), jnp.float32)
 
 
-def plane_scan(here_ref, blocks_ref, state_ref, map_ref, f_ref, b_ref):
+def plane_scan(reach_ref, blocks_ref, state_ref, map_ref, f_ref, b_ref):
     count = blocks_ref.shape[0]
     row = lax.broadcasted_iota(jnp.int32, (count, 128), 0)
     value = lambda n, some=slice(None): blocks_ref[some, n // 4, n % 4, :]
     v = [value(37 + n) for n in range(4)]
     below = jnp.where(row == 0, 0.0, pltpu.roll(v[3], 1, 0))
     above = jnp.where(row == count - 1, 0.0, pltpu.roll(v[0], count - 1, 0))
-    inverse = -1.0 / value(43)
+    here = blocks_ref[0, 10, 3:4, :]
+    reach = reach_ref[0:1, :]
+    for at in range(count):
+        reach = jnp.where(here == float(at), reach_ref[at % 4 : at % 4 + 1, :], reach)
+    inverse = -1.0 / reach
     for n, gradient in enumerate((0.5 * (v[1] - below), 0.5 * (above - v[2]))):
         map_ref[37 + n] = jnp.exp((1.0 + edge_slope * jnp.abs(gradient)) * inverse)
     for start in range(0, count, 8):
@@ -457,12 +462,12 @@
             b_ref[k, m : m + 1, :] = b[k]
         b = backward_out(block_at(m), [f_ref[k, m : m + 1, :] for k in range(4)], b)
 
-    here = here_ref[...]
+    here = jnp.broadcast_to(here, (4, 128))
 
     def mine(at):
         x = at(0)
         for g in range(1, count // 4):
-            x = jnp.where(here == g, at(g), x)
+            x = jnp.where(here > 4 * g - 0.5, at(g), x)
         return x
 
     for k in range(4):
@@ -492,10 +497,10 @@
     return lax.all_to_all(entering, axis, 0, 0, tiled=True)
 
 
-def states_by_planes(chunks, axis, group):
+def states_by_planes(chunks, axis, reach):
     size = lax.axis_size(axis)
     blocks = lax.all_to_all(chunks, axis, 0, 0, tiled=True)
-    entering = call(plane_scan, f32(4, 16, 128), [vmem(39, size, 128), vmem(4, size, 128), vmem(4, size, 128)], group, blocks)
+    entering = call(plane_scan, f32(4, 16, 128), [vmem(39, size, 128), vmem(4, size, 128), vmem(4, size, 128)], reach, blocks)
     fours = [[4 * g + i for i in range(4)] for g in range(size // 4)]
     return lax.all_to_all(entering, axis, 0, 0, axis_index_groups=fours, tiled=True)
 
@@ -505,7 +510,6 @@
         size = lax.axis_size(axis)
         return [f32(*padded), f32(37, 8, 128), f32(size, 11, 4, 128) if axis == "gy" else f32(size, SLOTS * 2 // size, 2, 128)]
 
-    group = jnp.full((4, 128), lax.shift_right_logical(lax.axis_index("gy"), 2), jnp.int32)
 
     work = [vmem(SLOTS * APART, 128)]
     ending = [vmem(*padded), vmem(STEPS, 8, 128), vmem(*padded), vmem(8 * APART, 128)]
@@ -517,7 +521,7 @@
     t, dy, y_half, y_chunks = call(
         x_second_y_first, [f32(*padded)] + maps("gy"), ending + work, vt, y_reach, source, dx, x_half, x_states
     )
-    y_states = states_by_planes(y_chunks, "gy", group)
+    y_states = states_by_planes(y_chunks, "gy", y_reach)
     out = call(y_second, f32(*plane), ending, t, dy, y_half, y_states)
     return out.reshape(4, 128, 128)
 

time: 71.6 us -> 70.6 us (0.986)
  blocking collectives: 36.2 us -> 63.5 us
  waiting for transfers between devices: 13.8 us -> 0 us
  starting transfers between devices: 13.6 us -> 0 us
  Pallas kernels: 6.59 us -> 5.85 us
    all_to_all x0 -> x1, blocking collectives: none -> 27.2 us  [states_by_planes(): blocks = lax.all_to_all(chunks, axis, 0, 0, tiled=True)]
    all_to_all x1 -> x0, waiting for transfers between devices: 13.8 us -> none  [states_by_planes(): blocks = lax.all_to_all(chunks, axis, 0, 0, tiled=True)]
    all_to_all x1 -> x0, starting transfers between devices: 13.6 us -> none  [states_by_planes(): blocks = lax.all_to_all(chunks, axis, 0, 0, tiled=True)]
    pallas_call x5, Pallas kernels: 6.59 us -> 5.85 us  [call(): pl.pallas_call(kernel, out_shape=out_shape, scratch_shapes=scratch, compi...]
  transfers between devices with their start and end apart: 1 -> 0, of which waited for: 1 -> 0; matrix products, arithmetic and copies ran while one was open for 0% -> 0% of each run, Pallas kernels for 0% -> 0%
where the time goes in v5:
time: 70.6 us; the launch traced here: 70.4 us
  blocking collectives  63.5 us (90%)
  Pallas kernels  5.85 us (8%)
  other arithmetic  1 us (1%)
    all_to_all x1, blocking collectives, states_by_planes(): blocks = lax.all_to_all(chunks, axis, 0, 0, tiled=True)  27.2 us
    all_to_all x1, blocking collectives, states(): chunks = lax.all_to_all(chunks, axis, 0, 0, tiled=True)  19.3 us
    all_to_all x1, blocking collectives, states(): return lax.all_to_all(entering, axis, 0, 0, tiled=True)  12.1 us
    pallas_call x5, Pallas kernels, call(): pl.pallas_call(kernel, out_shape=out_shape, scratch_shapes=scratch, compi...  5.85 us
    all_to_all x1, blocking collectives, states_by_planes(): lax.all_to_all(entering, axis, 0, 0, axis_index_groups=fours, tiled=True)  4.85 us

profile of v5, /device:TPU:1, one launch (start us, length us, event | category | flops | bytes accessed | tf_op | source)
XLA Modules:
  0.0 70.4 jit_solution(16273333956767792558)
XLA Ops:
  0.0 1.0 %pad_maximum_fusion.arguments_ref = f32[520,128]{1,0:T(8,128)S(1)} fusion(f32[4,128]{1,0:T(4,128)} %param.5, f32[4,128]{1,0:T(4,128)} %param.4, f32[512,128]{1,0:T(8,128)} %bitcast.2), kind=kLoop, calls=%fused_computation | loop fusion | flops 133120 | bytes 532480 | tf_op jit(solution)/shard_map/concatenate | solution.py:518
  1.0 1.5 %shard_map.37 = (f32[512,128]{1,0:T(8,128)S(1)}, f32[4,128]{1,0:T(4,128)S(1)}, f32[520,128]{1,0:T(8,128)S(1)}, f32[520,128]{1,0:T(8,128)S(1)}, f32[37,8,128]{2,1,0:T(8,128)S(1)}, /*index=5*/f32[32,3,2,128]{3,2,1,0:T(2,128)S(1)}) custom-call(f32[520,128]{1,0:T(8,128)S(1)} %pad_maximum_fusion.arguments_ref), custom_call_target="tpu_custom_call" | custom-call | tf_op jit(solution)/shard_map/pallas_call | solution.py:488
  2.5 19.3 %all_to_all.20.blocks_ref = f32[32,3,2,128]{3,2,1,0:T(2,128)S(1)} all-to-all(f32[32,3,2,128]{3,2,1,0:T(2,128)S(1)} %get-tuple-element.20), channel_id=1, replica_groups=mesh['gx'=32,'gy'=16] {'gx'}, dimensions={0} | all-to-all | bytes 196608 | tf_op jit(solution)/shard_map/all_to_all | solution.py:494
  21.8 0.8 %shard_map.38 = f32[32,2,128]{2,1,0:T(2,128)S(1)} custom-call(f32[32,3,2,128]{3,2,1,0:T(2,128)S(1)} %all_to_all.20.blocks_ref), custom_call_target="tpu_custom_call" | custom-call | tf_op jit(solution)/shard_map/pallas_call | solution.py:488
  22.6 12.1 %all_to_all.21.state_ref = f32[32,2,128]{2,1,0:T(2,128)S(1)} all-to-all(f32[32,2,128]{2,1,0:T(2,128)S(1)} %shard_map.38), channel_id=1, replica_groups=mesh['gx'=32,'gy'=16] {'gx'}, dimensions={0} | all-to-all | bytes 65536 | tf_op jit(solution)/shard_map/all_to_all | solution.py:497
  34.6 1.8 %shard_map.39 = (f32[520,128]{1,0:T(8,128)S(1)}, f32[520,128]{1,0:T(8,128)S(1)}, f32[37,8,128]{2,1,0:T(8,128)S(1)}, f32[16,11,4,128]{3,2,1,0:T(4,128)S(1)}) custom-call(f32[512,128]{1,0:T(8,128)S(1)} %get-tuple-element.15.vt_ref, f32[4,128]{1,0:T(4,128)S(1)} %get-tuple-element.16.reach_ref, f32[520,128]{1,0:T(8,128)S(1)} %get-tuple-element.17.source_ref, ...), custom_call_target="tpu_custom_call" | custom-call | tf_op jit(solution)/shard_map/pallas_call | solution.py:488
  36.5 27.2 %all_to_all.22.blocks_ref = f32[16,11,4,128]{3,2,1,0:T(4,128)S(1)} all-to-all(f32[16,11,4,128]{3,2,1,0:T(4,128)S(1)} %get-tuple-element.24), channel_id=1, replica_groups=mesh['gx'=32,'gy'=16] {'gy'}, dimensions={0} | all-to-all | bytes 720896 | tf_op jit(solution)/shard_map/all_to_all | solution.py:502
  63.7 0.5 shard_map.40
  64.2 4.8 %all_to_all.23.state_ref = f32[4,16,128]{2,1,0:T(8,128)S(1)} all-to-all(f32[4,16,128]{2,1,0:T(8,128)S(1)} %shard_map.40), channel_id=1, replica_groups={{0,1,2,3},{4,5,6,7},{8,9,10,11},{12,13,14,15},{16,17,18,19},{20,21,22,2..., dimensions={0} | all-to-all | bytes 65536 | tf_op jit(solution)/shard_map/all_to_all | solution.py:505
  69.1 1.3 %shard_map.41 = f32[512,128]{1,0:T(8,128)} custom-call(f32[520,128]{1,0:T(8,128)S(1)} %get-tuple-element.21.t_ref, f32[520,128]{1,0:T(8,128)S(1)} %get-tuple-element.22.d_ref, f32[37,8,128]{2,1,0:T(8,128)S(1)} %get-tuple-element.23.half_ref, f32[4,16,128]{2,1,0:T(8,128)S(1)} %all_to_all.23.state_ref), custom_call_target="tpu_custom_call" | custom-call | tf_op jit(solution)/shard_map/pallas_call | solution.py:488

commit v6 on v5

--- a/solution.py
+++ b/solution.py
@@ -118,14 +118,14 @@
 padded = (8 * PITCH, 128)
 
 
-def loop(body, carry, reverse=False):
+def loop(body, carry, reverse=False, unroll=UNROLL):
     def some(n, carry):
-        for k in range(UNROLL):
-            at = n * UNROLL + k
+        for k in range(unroll):
+            at = n * unroll + k
             carry = body(STEPS - 1 - at if reverse else at, carry)
         return carry
 
-    return lax.fori_loop(0, STEPS // UNROLL, some, carry)
+    return some(0, carry) if unroll == STEPS else lax.fori_loop(0, STEPS // unroll, some, carry)
 
 
 def rows(s):
@@ -290,7 +290,7 @@
         c_ref[s] = f[3]
         return f
 
-    loop(forward, f)
+    loop(forward, f, unroll=STEPS)
 
     def backward(s, b):
         p, q = poles_of(d_ref[rows(s), :])
@@ -298,7 +298,7 @@
         out_ref[rows(s), :] = b[3]
         return b
 
-    loop(backward, b, reverse=True)
+    loop(backward, b, reverse=True, unroll=STEPS)
 
 
 def x_first(arguments_ref, vt_ref, y_reach_ref, source_ref, d_ref, half_ref, chunks_ref, reach_ref, pair_ref):

time: 70.6 us -> 70.5 us (level)
  no operation moved by 1% of the time
where the time goes in v6:
time: 70.5 us; the launch traced here: 70.2 us
  blocking collectives  63.5 us (90%)
  Pallas kernels  5.72 us (8%)
  other arithmetic  1 us (1%)
    all_to_all x1, blocking collectives, states_by_planes(): blocks = lax.all_to_all(chunks, axis, 0, 0, tiled=True)  27.2 us
    all_to_all x1, blocking collectives, states(): chunks = lax.all_to_all(chunks, axis, 0, 0, tiled=True)  19.3 us
    all_to_all x1, blocking collectives, states(): return lax.all_to_all(entering, axis, 0, 0, tiled=True)  12.1 us
    pallas_call x5, Pallas kernels, call(): pl.pallas_call(kernel, out_shape=out_shape, scratch_shapes=scratch, compi...  5.72 us
    all_to_all x1, blocking collectives, states_by_planes(): lax.all_to_all(entering, axis, 0, 0, axis_index_groups=fours, tiled=True)  4.85 us

profile of v6, /device:TPU:1, one launch (start us, length us, event | category | flops | bytes accessed | tf_op | source)
XLA Modules:
  0.0 70.2 jit_solution(17580879553281092290)
XLA Ops:
  0.0 1.0 %pad_maximum_fusion.arguments_ref = f32[520,128]{1,0:T(8,128)S(1)} fusion(f32[4,128]{1,0:T(4,128)} %param.5, f32[4,128]{1,0:T(4,128)} %param.4, f32[512,128]{1,0:T(8,128)} %bitcast.2), kind=kLoop, calls=%fused_computation | loop fusion | flops 133120 | bytes 532480 | tf_op jit(solution)/shard_map/concatenate | solution.py:518
  1.0 1.5 %shard_map.37 = (f32[512,128]{1,0:T(8,128)S(1)}, f32[4,128]{1,0:T(4,128)S(1)}, f32[520,128]{1,0:T(8,128)S(1)}, f32[520,128]{1,0:T(8,128)S(1)}, f32[37,8,128]{2,1,0:T(8,128)S(1)}, /*index=5*/f32[32,3,2,128]{3,2,1,0:T(2,128)S(1)}) custom-call(f32[520,128]{1,0:T(8,128)S(1)} %pad_maximum_fusion.arguments_ref), custom_call_target="tpu_custom_call" | custom-call | tf_op jit(solution)/shard_map/pallas_call | solution.py:488
  2.5 19.3 %all_to_all.20.blocks_ref = f32[32,3,2,128]{3,2,1,0:T(2,128)S(1)} all-to-all(f32[32,3,2,128]{3,2,1,0:T(2,128)S(1)} %get-tuple-element.20), channel_id=1, replica_groups=mesh['gx'=32,'gy'=16] {'gx'}, dimensions={0} | all-to-all | bytes 196608 | tf_op jit(solution)/shard_map/all_to_all | solution.py:494
  21.8 0.8 %shard_map.38 = f32[32,2,128]{2,1,0:T(2,128)S(1)} custom-call(f32[32,3,2,128]{3,2,1,0:T(2,128)S(1)} %all_to_all.20.blocks_ref), custom_call_target="tpu_custom_call" | custom-call | tf_op jit(solution)/shard_map/pallas_call | solution.py:488
  22.6 12.1 %all_to_all.21.state_ref = f32[32,2,128]{2,1,0:T(2,128)S(1)} all-to-all(f32[32,2,128]{2,1,0:T(2,128)S(1)} %shard_map.38), channel_id=1, replica_groups=mesh['gx'=32,'gy'=16] {'gx'}, dimensions={0} | all-to-all | bytes 65536 | tf_op jit(solution)/shard_map/all_to_all | solution.py:497
  34.6 1.8 %shard_map.39 = (f32[520,128]{1,0:T(8,128)S(1)}, f32[520,128]{1,0:T(8,128)S(1)}, f32[37,8,128]{2,1,0:T(8,128)S(1)}, f32[16,11,4,128]{3,2,1,0:T(4,128)S(1)}) custom-call(f32[512,128]{1,0:T(8,128)S(1)} %get-tuple-element.15.vt_ref, f32[4,128]{1,0:T(4,128)S(1)} %get-tuple-element.16.reach_ref, f32[520,128]{1,0:T(8,128)S(1)} %get-tuple-element.17.source_ref, ...), custom_call_target="tpu_custom_call" | custom-call | tf_op jit(solution)/shard_map/pallas_call | solution.py:488
  36.4 27.2 %all_to_all.22.blocks_ref = f32[16,11,4,128]{3,2,1,0:T(4,128)S(1)} all-to-all(f32[16,11,4,128]{3,2,1,0:T(4,128)S(1)} %get-tuple-element.24), channel_id=1, replica_groups=mesh['gx'=32,'gy'=16] {'gy'}, dimensions={0} | all-to-all | bytes 720896 | tf_op jit(solution)/shard_map/all_to_all | solution.py:502
  63.7 0.5 shard_map.40
  64.2 4.8 %all_to_all.23.state_ref = f32[4,16,128]{2,1,0:T(8,128)S(1)} all-to-all(f32[4,16,128]{2,1,0:T(8,128)S(1)} %shard_map.40), channel_id=1, replica_groups={{0,1,2,3},{4,5,6,7},{8,9,10,11},{12,13,14,15},{16,17,18,19},{20,21,22,2..., dimensions={0} | all-to-all | bytes 65536 | tf_op jit(solution)/shard_map/all_to_all | solution.py:505
  69.0 1.2 %shard_map.41 = f32[512,128]{1,0:T(8,128)} custom-call(f32[520,128]{1,0:T(8,128)S(1)} %get-tuple-element.21.t_ref, f32[520,128]{1,0:T(8,128)S(1)} %get-tuple-element.22.d_ref, f32[37,8,128]{2,1,0:T(8,128)S(1)} %get-tuple-element.23.half_ref, f32[4,16,128]{2,1,0:T(8,128)S(1)} %all_to_all.23.state_ref), custom_call_target="tpu_custom_call" | custom-call | tf_op jit(solution)/shard_map/pallas_call | solution.py:488

commit v7 on v6

--- a/solution.py
+++ b/solution.py
@@ -113,7 +113,7 @@
     return p, [1.0 - x for x in p]
 
 
-STEPS, UNROLL = 64, 16
+STEPS, UNROLL = 64, 32
 PITCH = 65
 padded = (8 * PITCH, 128)
 

time: 70.5 us -> 70.4 us (level)
  no operation moved by 1% of the time
where the time goes in v7:
time: 70.4 us; the launch traced here: 70.2 us
  blocking collectives  63.5 us (90%)
  Pallas kernels  5.67 us (8%)
  other arithmetic  1 us (1%)
    all_to_all x1, blocking collectives, states_by_planes(): blocks = lax.all_to_all(chunks, axis, 0, 0, tiled=True)  27.2 us
    all_to_all x1, blocking collectives, states(): chunks = lax.all_to_all(chunks, axis, 0, 0, tiled=True)  19.3 us
    all_to_all x1, blocking collectives, states(): return lax.all_to_all(entering, axis, 0, 0, tiled=True)  12.1 us
    pallas_call x5, Pallas kernels, call(): pl.pallas_call(kernel, out_shape=out_shape, scratch_shapes=scratch, compi...  5.67 us
    all_to_all x1, blocking collectives, states_by_planes(): lax.all_to_all(entering, axis, 0, 0, axis_index_groups=fours, tiled=True)  4.85 us

profile of v7, /device:TPU:1, one launch (start us, length us, event | category | flops | bytes accessed | tf_op | source)
XLA Modules:
  0.0 70.2 jit_solution(11677394355504218021)
XLA Ops:
  0.0 1.0 %pad_maximum_fusion.arguments_ref = f32[520,128]{1,0:T(8,128)S(1)} fusion(f32[4,128]{1,0:T(4,128)} %param.5, f32[4,128]{1,0:T(4,128)} %param.4, f32[512,128]{1,0:T(8,128)} %bitcast.2), kind=kLoop, calls=%fused_computation | loop fusion | flops 133120 | bytes 532480 | tf_op jit(solution)/shard_map/concatenate | solution.py:518
  1.0 1.4 %shard_map.37 = (f32[512,128]{1,0:T(8,128)S(1)}, f32[4,128]{1,0:T(4,128)S(1)}, f32[520,128]{1,0:T(8,128)S(1)}, f32[520,128]{1,0:T(8,128)S(1)}, f32[37,8,128]{2,1,0:T(8,128)S(1)}, /*index=5*/f32[32,3,2,128]{3,2,1,0:T(2,128)S(1)}) custom-call(f32[520,128]{1,0:T(8,128)S(1)} %pad_maximum_fusion.arguments_ref), custom_call_target="tpu_custom_call" | custom-call | tf_op jit(solution)/shard_map/pallas_call | solution.py:488
  2.4 19.3 %all_to_all.20.blocks_ref = f32[32,3,2,128]{3,2,1,0:T(2,128)S(1)} all-to-all(f32[32,3,2,128]{3,2,1,0:T(2,128)S(1)} %get-tuple-element.20), channel_id=1, replica_groups=mesh['gx'=32,'gy'=16] {'gx'}, dimensions={0} | all-to-all | bytes 196608 | tf_op jit(solution)/shard_map/all_to_all | solution.py:494
  21.8 0.8 %shard_map.38 = f32[32,2,128]{2,1,0:T(2,128)S(1)} custom-call(f32[32,3,2,128]{3,2,1,0:T(2,128)S(1)} %all_to_all.20.blocks_ref), custom_call_target="tpu_custom_call" | custom-call | tf_op jit(solution)/shard_map/pallas_call | solution.py:488
  22.6 12.1 %all_to_all.21.state_ref = f32[32,2,128]{2,1,0:T(2,128)S(1)} all-to-all(f32[32,2,128]{2,1,0:T(2,128)S(1)} %shard_map.38), channel_id=1, replica_groups=mesh['gx'=32,'gy'=16] {'gx'}, dimensions={0} | all-to-all | bytes 65536 | tf_op jit(solution)/shard_map/all_to_all | solution.py:497
  34.6 1.7 %shard_map.39 = (f32[520,128]{1,0:T(8,128)S(1)}, f32[520,128]{1,0:T(8,128)S(1)}, f32[37,8,128]{2,1,0:T(8,128)S(1)}, f32[16,11,4,128]{3,2,1,0:T(4,128)S(1)}) custom-call(f32[512,128]{1,0:T(8,128)S(1)} %get-tuple-element.15.vt_ref, f32[4,128]{1,0:T(4,128)S(1)} %get-tuple-element.16.reach_ref, f32[520,128]{1,0:T(8,128)S(1)} %get-tuple-element.17.source_ref, ...), custom_call_target="tpu_custom_call" | custom-call | tf_op jit(solution)/shard_map/pallas_call | solution.py:488
  36.4 27.2 %all_to_all.22.blocks_ref = f32[16,11,4,128]{3,2,1,0:T(4,128)S(1)} all-to-all(f32[16,11,4,128]{3,2,1,0:T(4,128)S(1)} %get-tuple-element.24), channel_id=1, replica_groups=mesh['gx'=32,'gy'=16] {'gy'}, dimensions={0} | all-to-all | bytes 720896 | tf_op jit(solution)/shard_map/all_to_all | solution.py:502
  63.6 0.5 shard_map.40
  64.1 4.8 %all_to_all.23.state_ref = f32[4,16,128]{2,1,0:T(8,128)S(1)} all-to-all(f32[4,16,128]{2,1,0:T(8,128)S(1)} %shard_map.40), channel_id=1, replica_groups={{0,1,2,3},{4,5,6,7},{8,9,10,11},{12,13,14,15},{16,17,18,19},{20,21,22,2..., dimensions={0} | all-to-all | bytes 65536 | tf_op jit(solution)/shard_map/all_to_all | solution.py:505
  68.9 1.2 %shard_map.41 = f32[512,128]{1,0:T(8,128)} custom-call(f32[520,128]{1,0:T(8,128)S(1)} %get-tuple-element.21.t_ref, f32[520,128]{1,0:T(8,128)S(1)} %get-tuple-element.22.d_ref, f32[37,8,128]{2,1,0:T(8,128)S(1)} %get-tuple-element.23.half_ref, f32[4,16,128]{2,1,0:T(8,128)S(1)} %all_to_all.23.state_ref), custom_call_target="tpu_custom_call" | custom-call | tf_op jit(solution)/shard_map/pallas_call | solution.py:488
